TPU v7x, 128 devices: a whole 4x4x4 slice. The times are simulated.
128 devices in a mesh: row: 8 (over x_hi, z), col: 16 (over x_lo, y, core).
Axes of the slice: x: 4 (x_hi: 2, x_lo: 2; x = x_hi * 2 + x_lo), y: 4, z: 4, core: 2. Of those that a mesh axis runs over, the one named last changes fastest.
Arguments:
- three_index: bfloat16 [16384, 4096], P(('row', 'col')), may hold values from -0.59765625 to 0.59765625
- occ_index: int32 [4096], replicated, may hold values from 0 to 999
- vir_index: int32 [4096], replicated, may hold values from 0 to 3999
- occ_energy: float32 [1000], replicated, may hold values from -1.5 to -0.3
- vir_energy: float32 [4000], replicated, may hold values from 0.1 to 3
- frequency: float32 [1], replicated, may hold values from 0.3 to 2
Outputs:
- polar: float32 [16384, 8, 16, 128], P('row', None, 'col')
All inputs are finite; a program needn't handle non-finite values.
Results may differ from a plain program's by a relative error of at most 0.0026.
Values may be sent and summed in bfloat16 or wider, within the bound.
No kernel may reach another device: no remote copies, remote signals or barrier semaphores. Data moves between devices by JAX's collectives and lax.ppermute only.
A program may use at most 128 MiB of HBM per device.

v0:
```python
import jax
import jax.numpy as jnp
from jax import lax
from jax.sharding import PartitionSpec as P


def shards(three_index, occ_index, vir_index, occ_energy, vir_energy, frequency):
    gap = jnp.take(vir_energy, vir_index) - jnp.take(occ_energy, occ_index)
    denominator = -4.0 * gap / (gap * gap + frequency[0] * frequency[0])
    column_rows = lax.all_gather(three_index, "row", axis=0, tiled=True)
    n_col = lax.axis_size("col")
    own_rows = three_index.shape[0]
    slab = three_index.shape[1] // n_col
    regrouped = lax.all_to_all(three_index, "col", split_axis=1, concat_axis=0, tiled=True)
    my_denominator = lax.dynamic_slice_in_dim(denominator, lax.axis_index("col") * slab, slab, 0)
    panel = (regrouped.astype(jnp.float32) * my_denominator[None, :]).astype(jnp.bfloat16)
    tile = lax.dot_general(
        lax.all_gather(panel, "col", axis=1, tiled=True),
        column_rows,
        (((1,), (1,)), ((), ())),
        preferred_element_type=jnp.float32,
    )
    n_row = column_rows.shape[0] // own_rows
    return tile.reshape(tile.shape[0], n_row, 1, own_rows)


def solution(mesh):
    placed = (P(("row", "col"), None), P(), P(), P(), P(), P())
    return jax.shard_map(
        shards, mesh=mesh, in_specs=placed, out_specs=P("row", None, "col", None), check_vma=False
    )
```

profile of v0, /device:TPU:1, one launch (start us, length us, event | category | flops | bytes accessed | tf_op | source)
XLA Modules:
  0.0 276.5 jit_solution(7278398339701349888)
XLA Ops:
  6.5 0.0 copy-start
  6.5 0.0 all-gather.5.cloned.1.call-start
  6.5 0.7 all-gather.5.cloned.1.call-update
  7.3 2.3 copy.9
  9.5 6.9 %all-to-all-start = ((bf16[128,16,256]{0,2,1:T(8,128)(2,1)}), bf16[128,16,256]{0,2,1:T(8,128)(2,1)S(1)}, u32[]{:S(2)}, u32[]{:S(2)}) async-start(bf16[128,16,256]{0,2,1:T(8,128)(2,1)} %bitcast), calls=%async_computation | async-start | bytes 2097152 | tf_op jit(solution)/shard_map/all_to_all | solution.py:14
  16.4 0.0 all-gather.3.cloned.1.call-start
  17.1 0.7 fusion.4
  17.9 0.0 copy-done.1
  17.9 16.7 %gather_fusion.1 = f32[4096]{0:T(1024)S(1)} fusion(f32[1000]{0:T(1024)S(1)} %copy-done.1, s32[4096]{0:T(1024)S(1)} %fusion.4), kind=kCustom, calls=%fused_computation.1 | custom fusion | bytes 49152 | tf_op jit(solution)/shard_map/jit(_take)/gather | solution.py:8
  34.6 0.0 copy-done.3
  34.6 0.0 copy-done
  34.6 0.0 copy-start.2
  34.6 23.0 %gather_fusion = f32[4096]{0:T(1024)S(1)} fusion(f32[4000]{0:T(1024)S(1)} %copy-done, s32[4096]{0:T(1024)S(1)} %fusion.1), kind=kCustom, calls=%fused_computation | custom fusion | bytes 49152 | tf_op jit(solution)/shard_map/jit(_take)/gather | solution.py:8
  57.6 0.0 copy-done.2
  57.7 0.1 add_divide_fusion
  57.8 0.0 all-to-all-done
  57.8 1.5 convert_bitcast_fusion
  59.3 1.9 copy.10
  61.2 1.2 fusion
  62.4 0.0 all-gather.3.cloned.1.call-update
  62.4 63.0 %all-gather.5.cloned.1.call-done = bf16[1024,4096]{1,0:T(8,128)(2,1)} async-done(((bf16[128,4096]{1,0:T(8,128)(2,1)}), bf16[1024,4096]{1,0:T(8,128)(2,1)}) %all-gather.5.cloned.1.call-update) | async-done | bytes 8388624 | tf_op jit(solution)/shard_map/all_gather | solution.py:10
  125.4 99.6 %all-gather.3.cloned.1.call-done = bf16[2048,4096]{1,0:T(8,128)(2,1)} async-done(((bf16[2048,256]{1,0:T(8,128)(2,1)}), bf16[2048,4096]{1,0:T(8,128)(2,1)}) %all-gather.3.cloned.1.call-update) | async-done | bytes 16777232 | tf_op jit(solution)/shard_map/all_gather | solution.py:18
  225.0 24.2 %fusion.10 = f32[2048,1024]{0,1:T(8,128)} fusion(bf16[2048,4096]{1,0:T(8,128)(2,1)} %all-gather.3.cloned.1.call-done, bf16[1024,4096]{1,0:T(8,128)(2,1)} %all-gather.5.cloned.1.call-done), kind=kOutput, calls=%fused_computation.19 | convolution fusion | flops 17179869184 | bytes 33554432 | tf_op jit(solution)/shard_map/dot_general | solution.py:17
  249.2 20.5 %copy.11 = f32[2048,8,1,128]{3,2,1,0:T(1,128)} copy(f32[2048,8,1,128]{0,3,1,2:T(8,128)} %bitcast.11) | data formatting | bytes 16777216 | tf_op jit(solution)/shard_map/reshape | solution.py:24
  (4 shorter events, 0.0 us)
Async XLA Ops:
  6.5 28.1 %copy-start = (f32[4000]{0:T(1024)S(1)}, f32[4000]{0:T(1024)}, u32[]{:S(2)}) copy-start(f32[4000]{0:T(1024)} %param.10) | copy-start | bytes 48004
  6.5 11.3 %copy-start.1 = (f32[1000]{0:T(1024)S(1)}, f32[1000]{0:T(1024)}, u32[]{:S(2)}) copy-start(f32[1000]{0:T(1024)} %param.9) | copy-start | bytes 12004
  6.5 118.9 %all-gather.5.cloned.1.call-start = ((), (), s32[]{:S(2)}) async-start(), calls=%async_computation.2 | async-start | bytes 9437184 | tf_op jit(solution)/shard_map/all_gather | solution.py:10
  9.5 48.3 %all-to-all-start = ((bf16[128,16,256]{0,2,1:T(8,128)(2,1)}), bf16[128,16,256]{0,2,1:T(8,128)(2,1)S(1)}, u32[]{:S(2)}, u32[]{:S(2)}) async-start(bf16[128,16,256]{0,2,1:T(8,128)(2,1)} %bitcast), calls=%async_computation | async-start | bytes 2097152 | tf_op jit(solution)/shard_map/all_to_all | solution.py:14
  16.4 208.6 %all-gather.3.cloned.1.call-start = ((), (), s32[]{:S(2)}) async-start(), calls=%async_computation.1 | async-start | bytes 17825792 | tf_op jit(solution)/shard_map/all_gather | solution.py:18
  17.9 16.7 %copy-start.3 = (s32[4096]{0:T(1024)S(1)}, s32[4096]{0:T(1024)}, u32[]{:S(2)}) copy-start(s32[4096]{0:T(1024)} %param.8) | copy-start | bytes 49156
  34.6 23.1 %copy-start.2 = (s32[4096]{0:T(1024)S(1)}, s32[4096]{0:T(1024)}, u32[]{:S(2)}) copy-start(s32[4096]{0:T(1024)} %param.7) | copy-start | bytes 49156
Sparse Core Ops, SparseCore 0:
  9.7 115.6 all-gather.4
  127.0 97.9 all-gather.2
where the time goes:
time: 277 us
  waiting for transfers between devices  163 us (59%)
  local copies, waits for them, and re-layouts  64.4 us (23%)
  matrix products  24.2 us (9%)
  between operations  14.1 us (5%)
  starting transfers between devices  6.95 us (3%)
  other arithmetic  3.52 us (1%)
    all_gather x1, waiting for transfers between devices, shards(): lax.all_gather(panel, 'col', axis=1, tiled=True)  99.6 us
    all_gather x1, waiting for transfers between devices, shards(): column_rows = lax.all_gather(three_index, 'row', axis=0, tiled=True)  63 us
    gather x2, local copies, waits for them, and re-layouts, shards(): gap = jnp.take(vir_energy, vir_index) - jnp.take(occ_energy, occ_index)  39.7 us
    dot_general x1, matrix products, shards(): lax.dot_general(lax.all_gather(panel, 'col', axis=1, tiled=True), column_...  24.2 us
    reshape x1, local copies, waits for them, and re-layouts, shards(): return tile.reshape(tile.shape[0], n_row, 1, own_rows)  20.5 us
    all_to_all x1, starting transfers between devices, shards(): lax.all_to_all(three_index, 'col', split_axis=1, concat_axis=0, tiled=True)  6.91 us
  transfers between devices with their start and end apart: 3, of which 2 were waited for; matrix products, arithmetic and copies ran while one was open for 17% of the time, Pallas kernels for 0%

commit v1 on v0

v1 whole, which is shorter than its diff:
```python
import jax
import jax.numpy as jnp
from jax import lax
from jax.experimental import pallas as pl
from jax.experimental.pallas import tpu as pltpu
from jax.sharding import PartitionSpec as P

NT = (((1,), (1,)), ((), ()))
LANES = 128
N_ROW, N_COL = 8, 16
FIRST = 96


def z_ring():
    pairs = []
    for r in range(N_ROW):
        for c in range(N_COL):
            z = (r % 4 + (1 if c % 2 == 0 else -1)) % 4
            pairs.append((r * N_COL + c, (r // 4 * 4 + z) * N_COL + c))
    return pairs


def other_x():
    return [(r, (r + 4) % N_ROW) for r in range(N_ROW)]


def scale(three_index, occ_index, vir_index, occ_energy, vir_energy, frequency, cuts):
    rows, pairs = three_index.shape
    chunks = pairs // LANES

    def table(energy):
        padded = -(-energy.shape[0] // (8 * LANES)) * 8 * LANES
        return jnp.pad(energy, (0, padded - energy.shape[0])).reshape(-1, LANES)

    def kernel(freq, occ, vir, occ_table, vir_table, b, *outs):
        def look_up(table_ref, index):
            high, low = index >> 7, index & (LANES - 1)
            found = jnp.zeros(index.shape, jnp.float32)
            for k in range(table_ref.shape[0]):
                line = jnp.broadcast_to(table_ref[k : k + 1, :], index.shape)
                found = jnp.where(high == k, jnp.take_along_axis(line, low, axis=1), found)
            return found

        gap = look_up(vir_table, vir[...]) - look_up(occ_table, occ[...])
        denominator = -4.0 * gap / (gap * gap + freq[0] * freq[0])
        for k in range(chunks):
            at = slice(k * LANES, (k + 1) * LANES)
            scaled = (b[:, at].astype(jnp.float32) * denominator[k : k + 1, :]).astype(jnp.bfloat16)
            start = 0
            for out in outs:
                out[:, at] = scaled[start : start + out.shape[0]]
                start += out.shape[0]

    vmem = pl.BlockSpec(memory_space=pltpu.VMEM)
    return pl.pallas_call(
        kernel,
        out_shape=[jax.ShapeDtypeStruct((n, pairs), jnp.bfloat16) for n in cuts],
        in_specs=[pl.BlockSpec(memory_space=pltpu.SMEM)] + [vmem] * 5,
        out_specs=[vmem] * len(cuts),
        compiler_params=pltpu.CompilerParams(vmem_limit_bytes=32 << 20),
    )(
        frequency,
        occ_index.reshape(chunks, LANES),
        vir_index.reshape(chunks, LANES),
        table(occ_energy),
        table(vir_energy),
        three_index,
    )


def multiply(a, pieces, places, out, offset, group):
    r = a.shape[0] // N_COL
    depth = a.shape[1]
    m = group * r
    tiles = N_COL // group
    n_pieces = len(pieces)
    pr = pieces[0].shape[0]
    width = 2 * LANES
    n_wide = N_ROW * LANES // width

    def kernel(*refs):
        place = refs[0]
        a_ref, j_refs = refs[1], refs[2 : 2 + n_pieces]
        o, j_all, a_buf, acc, j_sem, a_sem, o_sem = refs[-7:]
        loads = []
        for j in range(n_pieces):
            to = pl.multiple_of(place[j], pr)
            loads.append(pltpu.make_async_copy(j_refs[j], j_all.at[pl.ds(to, pr)], j_sem.at[j]))
            loads[-1].start()

        def load(t):
            return pltpu.make_async_copy(a_ref.at[pl.ds(t * m, m)], a_buf.at[t % 2], a_sem.at[t % 2])

        load(0).start()
        for c in loads:
            c.wait()
        pending = [[], []]
        for t in range(tiles):
            load(t).wait()
            if t + 1 < tiles:
                load(t + 1).start()
            for w in range(n_wide):
                slot = (t * n_wide + w) % 2
                for c in pending[slot]:
                    c.wait()
                tile = lax.dot_general(
                    a_buf[t % 2], j_all[w * width : (w + 1) * width, :], NT, preferred_element_type=jnp.float32
                )
                acc[slot] = tile.reshape(group, r, width)
                pending[slot] = []
                for h in range(2):
                    c = pltpu.make_async_copy(
                        acc.at[slot, :, :, h * LANES : (h + 1) * LANES],
                        o.at[t * group : (t + 1) * group, offset : offset + r, 2 * w + h, 0, :],
                        o_sem.at[slot, h],
                    )
                    c.start()
                    pending[slot].append(c)
        for p in pending:
            for c in p:
                c.wait()

    hbm = pl.BlockSpec(memory_space=pl.ANY)
    has = out is not None
    return pl.pallas_call(
        kernel,
        out_shape=jax.ShapeDtypeStruct((N_COL, LANES, N_ROW, 1, LANES), jnp.float32),
        in_specs=[pl.BlockSpec(memory_space=pltpu.SMEM)] + [hbm] * (1 + n_pieces + has),
        out_specs=hbm,
        input_output_aliases={2 + n_pieces: 0} if has else {},
        scratch_shapes=[
            pltpu.VMEM((N_ROW * LANES, depth), jnp.bfloat16),
            pltpu.VMEM((2, m, depth), jnp.bfloat16),
            pltpu.VMEM((2, group, r, width), jnp.float32),
            pltpu.SemaphoreType.DMA((n_pieces,)),
            pltpu.SemaphoreType.DMA((2,)),
            pltpu.SemaphoreType.DMA((2, 2)),
        ],
        compiler_params=pltpu.CompilerParams(vmem_limit_bytes=40 << 20),
        cost_estimate=pl.CostEstimate(
            flops=2 * a.shape[0] * N_ROW * LANES * depth, bytes_accessed=24 << 20, transcendentals=0
        ),
    )(places, a, *pieces, *([out] if has else []))


def after(value, *earlier):
    return lax.optimization_barrier((value,) + earlier)[0]


def shards(three_index, occ_index, vir_index, occ_energy, vir_energy, frequency):
    own = three_index.shape[0]
    cuts = (FIRST, own - FIRST)
    scaled = scale(three_index, occ_index, vir_index, occ_energy, vir_energy, frequency, cuts)
    first = lax.all_gather(scaled[0], "col", axis=0, tiled=True)
    second = lax.all_gather(scaled[1], "col", axis=0, tiled=True)

    ring = z_ring()
    half = own // 2
    mine = [three_index[:half], three_index[half:]]
    step = lambda block: lax.ppermute(block, ("row", "col"), ring)
    quarter = half // 2
    cross = [lax.ppermute(mine[0], "row", other_x())]
    for p in range(2):
        part = three_index[half + p * quarter : half + (p + 1) * quarter]
        cross.append(lax.ppermute(after(part, cross[-1]), "row", other_x()))
    near = [[m] for m in mine]
    for h in range(2):
        for _ in range(3):
            near[h].append(step(near[h][-1]))
    far = [[after(cross[0], near[0][3])], [after(jnp.concatenate(cross[1:], 0), near[1][3])]]
    for h in range(2):
        for _ in range(3):
            far[h].append(step(far[h][-1]))

    row, core = lax.axis_index("row"), lax.axis_index("col") % 2
    x_hi, z = row // 4, row % 4
    toward = 1 - 2 * core
    pieces, places = [], []
    for h in range(2):
        for i in range(4):
            for blocks, x in ((near, x_hi), (far, 1 - x_hi)):
                pieces.append(blocks[h][i])
                places.append((x * 4 + (z - i * toward) % 4) * own + h * half)
    places = jnp.stack(places).astype(jnp.int32)
    out = multiply(first, pieces, places, None, 0, 4)
    out = multiply(second, pieces, places, out, FIRST, 16)
    return out.reshape(N_COL * own, N_ROW, 1, own)


def solution(mesh):
    placed = (P(("row", "col"), None), P(), P(), P(), P(), P())
    return jax.shard_map(
        shards, mesh=mesh, in_specs=placed, out_specs=P("row", None, "col", None), check_vma=False
    )
```

time: 277 us -> 182 us (0.66)
  the two profiles are of different devices: /device:TPU:1 before, /device:TPU:28 now
where the time goes in v1:
time: 182 us; the launch traced here: 181 us
  waiting for transfers between devices  84.1 us (46%)
  Pallas kernels  47.8 us (26%)
  local copies, waits for them, and re-layouts  24.5 us (13%)
  between operations  14.2 us (8%)
  starting transfers between devices  10.1 us (6%)
    pallas_call x2, Pallas kernels, multiply(): pl.pallas_call(kernel, out_shape=jax.ShapeDtypeStruct((N_COL, LANES, N_RO...  46 us
    ppermute x12, waiting for transfers between devices, shards(): step = lambda block: lax.ppermute(block, ('row', 'col'), ring)  44.8 us
    ppermute x2, waiting for transfers between devices, shards(): cross.append(lax.ppermute(after(part, cross[-1]), 'row', other_x()))  27.6 us
    unnamed x44, local copies, waits for them, and re-layouts  20.7 us
    ppermute x1, waiting for transfers between devices, shards(): cross = [lax.ppermute(mine[0], 'row', other_x())]  11 us
    ppermute x12, starting transfers between devices, shards(): step = lambda block: lax.ppermute(block, ('row', 'col'), ring)  9.43 us
  transfers between devices with their start and end apart: 17, of which 11 were waited for; matrix products, arithmetic and copies ran while one was open for 1% of the time, Pallas kernels for 18%

profile of v1, /device:TPU:28, one launch (start us, length us, event | category | flops | bytes accessed | tf_op | source)
XLA Modules:
  0.0 180.7 jit_solution(2899510528482042142)
XLA Ops:
  8.6 1.2 copy-done
  11.3 1.8 shard_map.64
  13.8 1.3 fusion.1
  15.1 2.0 %collective-permute-start.9 = (bf16[64,4096]{1,0:T(8,128)(2,1)S(1)}, bf16[64,4096]{1,0:T(8,128)(2,1)S(1)}, u32[]{:S(2)}, u32[]{:S(2)}) collective-permute-start(bf16[64,4096]{1,0:T(8,128)(2,1)S(1)} %get-tuple-element.19.refs_10_), channel_id=1, source_target_pairs={{0,16},{1,49},{2,18},{3,51},{4,20},{5,53},{6,22},{7,55},{8,24},{9,... | collective-permute-start | bytes 1572872 | tf_op jit(solution)/shard_map/ppermute | solution.py:160
  17.1 1.9 %collective-permute-start.1 = (bf16[64,4096]{1,0:T(8,128)(2,1)S(1)}, bf16[64,4096]{1,0:T(8,128)(2,1)S(1)}, u32[]{:S(2)}, u32[]{:S(2)}) collective-permute-start(bf16[64,4096]{1,0:T(8,128)(2,1)S(1)} %get-tuple-element.20.refs_2_), channel_id=1, source_target_pairs={{0,16},{1,49},{2,18},{3,51},{4,20},{5,53},{6,22},{7,55},{8,24},{9,... | collective-permute-start | bytes 1572872 | tf_op jit(solution)/shard_map/ppermute | solution.py:160
  19.5 6.9 %collective-permute-done.9.refs_12_ = bf16[64,4096]{1,0:T(8,128)(2,1)S(1)} collective-permute-done((bf16[64,4096]{1,0:T(8,128)(2,1)S(1)}, bf16[64,4096]{1,0:T(8,128)(2,1)S(1)}, u32[]{:S(2)}, u32[]{:S(2)}) %collective-permute-start.9) | collective-permute-done | bytes 524320 | tf_op jit(solution)/shard_map/ppermute | solution.py:160
  26.4 5.6 %collective-permute-done.1.refs_4_ = bf16[64,4096]{1,0:T(8,128)(2,1)S(1)} collective-permute-done((bf16[64,4096]{1,0:T(8,128)(2,1)S(1)}, bf16[64,4096]{1,0:T(8,128)(2,1)S(1)}, u32[]{:S(2)}, u32[]{:S(2)}) %collective-permute-start.1) | collective-permute-done | bytes 524320 | tf_op jit(solution)/shard_map/ppermute | solution.py:160
  32.0 1.1 fusion
  33.1 11.0 %collective-permute-done.refs_3_ = bf16[64,4096]{1,0:T(8,128)(2,1)S(1)} collective-permute-done((bf16[64,4096]{1,0:T(8,128)(2,1)S(1)}, bf16[64,4096]{1,0:T(8,128)(2,1)S(1)}, u32[]{:S(2)}, u32[]{:S(2)}) %collective-permute-start) | collective-permute-done | bytes 524320 | tf_op jit(solution)/shard_map/ppermute | solution.py:162
  44.0 14.9 %collective-permute-done.7 = bf16[32,4096]{1,0:T(8,128)(2,1)S(1)} collective-permute-done((bf16[32,4096]{1,0:T(8,128)(2,1)S(1)}, bf16[32,4096]{1,0:T(8,128)(2,1)S(1)}, u32[]{:S(2)}, u32[]{:S(2)}) %collective-permute-start.7) | collective-permute-done | bytes 262176 | tf_op jit(solution)/shard_map/ppermute | solution.py:165
  59.0 1.7 collective-permute-start.11
  60.8 12.7 %collective-permute-done.8 = bf16[32,4096]{1,0:T(8,128)(2,1)S(1)} collective-permute-done((bf16[32,4096]{1,0:T(8,128)(2,1)S(1)}, bf16[32,4096]{1,0:T(8,128)(2,1)S(1)}, u32[]{:S(2)}, u32[]{:S(2)}) %collective-permute-start.8) | collective-permute-done | bytes 262176 | tf_op jit(solution)/shard_map/ppermute | solution.py:165
  74.3 1.7 collective-permute-start.12
  76.9 7.9 %collective-permute-done.12.refs_13_ = bf16[64,4096]{1,0:T(8,128)(2,1)S(1)} collective-permute-done((bf16[64,4096]{1,0:T(8,128)(2,1)S(1)}, bf16[64,4096]{1,0:T(8,128)(2,1)S(1)}, u32[]{:S(2)}, u32[]{:S(2)}) %collective-permute-start.12) | collective-permute-done | bytes 524320 | tf_op jit(solution)/shard_map/ppermute | solution.py:160
  86.0 4.3 %collective-permute-done.4.refs_5_ = bf16[64,4096]{1,0:T(8,128)(2,1)S(1)} collective-permute-done((bf16[64,4096]{1,0:T(8,128)(2,1)S(1)}, bf16[64,4096]{1,0:T(8,128)(2,1)S(1)}, u32[]{:S(2)}, u32[]{:S(2)}) %collective-permute-start.4) | collective-permute-done | bytes 524320 | tf_op jit(solution)/shard_map/ppermute | solution.py:160
  91.7 4.4 %collective-permute-done.13.refs_15_ = bf16[64,4096]{1,0:T(8,128)(2,1)} collective-permute-done((bf16[64,4096]{1,0:T(8,128)(2,1)S(1)}, bf16[64,4096]{1,0:T(8,128)(2,1)}, u32[]{:S(2)}, u32[]{:S(2)}) %collective-permute-start.13) | collective-permute-done | bytes 524320 | tf_op jit(solution)/shard_map/ppermute | solution.py:160
  96.6 5.1 %collective-permute-done.5.refs_7_ = bf16[64,4096]{1,0:T(8,128)(2,1)} collective-permute-done((bf16[64,4096]{1,0:T(8,128)(2,1)S(1)}, bf16[64,4096]{1,0:T(8,128)(2,1)}, u32[]{:S(2)}, u32[]{:S(2)}) %collective-permute-start.5) | collective-permute-done | bytes 524320 | tf_op jit(solution)/shard_map/ppermute | solution.py:160
  102.3 5.0 %collective-permute-done.14.refs_17_ = bf16[64,4096]{1,0:T(8,128)(2,1)} collective-permute-done((bf16[64,4096]{1,0:T(8,128)(2,1)}, bf16[64,4096]{1,0:T(8,128)(2,1)}, u32[]{:S(2)}, u32[]{:S(2)}) %collective-permute-start.14) | collective-permute-done | bytes 524320 | tf_op jit(solution)/shard_map/ppermute | solution.py:160
  107.3 5.6 %collective-permute-done.6.refs_9_ = bf16[64,4096]{1,0:T(8,128)(2,1)} collective-permute-done((bf16[64,4096]{1,0:T(8,128)(2,1)}, bf16[64,4096]{1,0:T(8,128)(2,1)}, u32[]{:S(2)}, u32[]{:S(2)}) %collective-permute-start.6) | collective-permute-done | bytes 524320 | tf_op jit(solution)/shard_map/ppermute | solution.py:160
  112.9 1.0 copy-done.3
  115.0 1.1 copy-done.9
  119.3 33.3 %shard_map.65.refs_18_ = f32[16,128,8,1,128]{4,3,2,1,0:T(1,128)} custom-call(s32[16]{0:T(128)S(1)} %stack.67.refs_0_, bf16[1536,4096]{1,0:T(8,128)(2,1)} %all-gather.5.cloned.1.call-done.refs_1_, bf16[64,4096]{1,0:T(8,128)(2,1)S(1)} %get-tuple-element.20.refs_2_, bf16[64,4096]{1,0:T(8,128)(2,1)S(1)} %collective-permute-done.refs_3_, ...), custom_call_target="tpu_custom_call" | custom-call | flops 12884901888 | bytes 25165824 | tf_op jit(solution)/shard_map/pallas_call | solution.py:125
  152.7 2.2 %copy-done.1 = bf16[512,4096]{1,0:T(8,128)(2,1)S(1)} copy-done((bf16[512,4096]{1,0:T(8,128)(2,1)S(1)}, bf16[512,4096]{1,0:T(8,128)(2,1)}, u32[]{:S(2)}) %copy-start.1) | copy-done | bytes 4194328
  161.1 12.7 %shard_map.66 = f32[16,128,8,1,128]{4,3,2,1,0:T(1,128)} custom-call(s32[16]{0:T(128)S(1)} %stack.67.refs_0_, bf16[512,4096]{1,0:T(8,128)(2,1)S(1)} %copy-done.1, bf16[64,4096]{1,0:T(8,128)(2,1)S(1)} %get-tuple-element.20.refs_2_, bf16[64,4096]{1,0:T(8,128)(2,1)S(1)} %collective-permute-done.refs_3_, ...), custom_call_target="tpu_custom_call", output_to_operand_aliasing={{}: (18, {})} | custom-call | flops 4294967296 | bytes 25165824 | tf_op jit(solution)/shard_map/pallas_call | solution.py:125
  (65 shorter events, 20.1 us)
Async XLA Ops:
  6.5 106.4 %all-gather.5.cloned.1.call-start = ((), (), s32[]{:S(2)}) async-start(), calls=%async_computation.1 | async-start | bytes 13369344 | tf_op jit(solution)/shard_map/all_gather | solution.py:154
  8.6 1.2 copy-start
  13.1 139.6 %all-gather.3.cloned.1.call-start = ((), (), s32[]{:S(2)}) async-start(), calls=%async_computation | async-start | bytes 4456448 | tf_op jit(solution)/shard_map/all_gather | solution.py:155
  15.1 11.3 %collective-permute-start.9 = (bf16[64,4096]{1,0:T(8,128)(2,1)S(1)}, bf16[64,4096]{1,0:T(8,128)(2,1)S(1)}, u32[]{:S(2)}, u32[]{:S(2)}) collective-permute-start(bf16[64,4096]{1,0:T(8,128)(2,1)S(1)} %get-tuple-element.19.refs_10_), channel_id=1, source_target_pairs={{0,16},{1,49},{2,18},{3,51},{4,20},{5,53},{6,22},{7,55},{8,24},{9,... | collective-permute-start | bytes 1572872 | tf_op jit(solution)/shard_map/ppermute | solution.py:160
  17.1 14.9 %collective-permute-start.1 = (bf16[64,4096]{1,0:T(8,128)(2,1)S(1)}, bf16[64,4096]{1,0:T(8,128)(2,1)S(1)}, u32[]{:S(2)}, u32[]{:S(2)}) collective-permute-start(bf16[64,4096]{1,0:T(8,128)(2,1)S(1)} %get-tuple-element.20.refs_2_), channel_id=1, source_target_pairs={{0,16},{1,49},{2,18},{3,51},{4,20},{5,53},{6,22},{7,55},{8,24},{9,... | collective-permute-start | bytes 1572872 | tf_op jit(solution)/shard_map/ppermute | solution.py:160
  19.0 25.0 %collective-permute-start = (bf16[64,4096]{1,0:T(8,128)(2,1)S(1)}, bf16[64,4096]{1,0:T(8,128)(2,1)S(1)}, u32[]{:S(2)}, u32[]{:S(2)}) collective-permute-start(bf16[64,4096]{1,0:T(8,128)(2,1)S(1)} %get-tuple-element.20.refs_2_), channel_id=1, source_target_pairs={{0,64},{16,80},{32,96},{48,112},{64,0},{80,16},{96,32},{112,48},{1... | collective-permute-start | bytes 1572872 | tf_op jit(solution)/shard_map/ppermute | solution.py:162
  26.4 32.6 %collective-permute-start.10 = (bf16[64,4096]{1,0:T(8,128)(2,1)S(1)}, bf16[64,4096]{1,0:T(8,128)(2,1)S(1)}, u32[]{:S(2)}, u32[]{:S(2)}) collective-permute-start(bf16[64,4096]{1,0:T(8,128)(2,1)S(1)} %collective-permute-done.9.refs_12_), channel_id=1, source_target_pairs={{0,16},{1,49},{2,18},{3,51},{4,20},{5,53},{6,22},{7,55},{8,24},{9,... | collective-permute-start | bytes 1572872 | tf_op jit(solution)/shard_map/ppermute | solution.py:160
  32.0 28.7 %collective-permute-start.2 = (bf16[64,4096]{1,0:T(8,128)(2,1)S(1)}, bf16[64,4096]{1,0:T(8,128)(2,1)S(1)}, u32[]{:S(2)}, u32[]{:S(2)}) collective-permute-start(bf16[64,4096]{1,0:T(8,128)(2,1)S(1)} %collective-permute-done.1.refs_4_), channel_id=1, source_target_pairs={{0,16},{1,49},{2,18},{3,51},{4,20},{5,53},{6,22},{7,55},{8,24},{9,... | collective-permute-start | bytes 1572872 | tf_op jit(solution)/shard_map/ppermute | solution.py:160
  44.0 14.9 %collective-permute-start.7 = (bf16[32,4096]{1,0:T(8,128)(2,1)S(1)}, bf16[32,4096]{1,0:T(8,128)(2,1)S(1)}, u32[]{:S(2)}, u32[]{:S(2)}) collective-permute-start(bf16[32,4096]{1,0:T(8,128)(2,1)S(1)} %get-tuple-element.13), channel_id=1, source_target_pairs={{0,64},{16,80},{32,96},{48,112},{64,0},{80,16},{96,32},{112,48},{1... | collective-permute-start | bytes 786440 | tf_op jit(solution)/shard_map/ppermute | solution.py:165
  58.9 14.6 %collective-permute-start.8 = (bf16[32,4096]{1,0:T(8,128)(2,1)S(1)}, bf16[32,4096]{1,0:T(8,128)(2,1)S(1)}, u32[]{:S(2)}, u32[]{:S(2)}) collective-permute-start(bf16[32,4096]{1,0:T(8,128)(2,1)S(1)} %get-tuple-element.14), channel_id=1, source_target_pairs={{0,64},{16,80},{32,96},{48,112},{64,0},{80,16},{96,32},{112,48},{1... | collective-permute-start | bytes 786440 | tf_op jit(solution)/shard_map/ppermute | solution.py:165
  59.0 31.4 %copy-start.2 = (bf16[64,4096]{1,0:T(8,128)(2,1)}, bf16[64,4096]{1,0:T(8,128)(2,1)S(1)}, u32[]{:S(2)}) copy-start(bf16[64,4096]{1,0:T(8,128)(2,1)S(1)} %collective-permute-done.10.refs_14_) | copy-start | bytes 1572868
  59.0 14.5 %collective-permute-start.11 = (bf16[64,4096]{1,0:T(8,128)(2,1)S(1)}, bf16[64,4096]{1,0:T(8,128)(2,1)S(1)}, u32[]{:S(2)}, u32[]{:S(2)}) collective-permute-start(bf16[64,4096]{1,0:T(8,128)(2,1)S(1)} %collective-permute-done.10.refs_14_), channel_id=1, source_target_pairs={{0,16},{1,49},{2,18},{3,51},{4,20},{5,53},{6,22},{7,55},{8,24},{9,... | collective-permute-start | bytes 1572872 | tf_op jit(solution)/shard_map/ppermute | solution.py:160
  60.7 30.1 %copy-start.5 = (bf16[64,4096]{1,0:T(8,128)(2,1)}, bf16[64,4096]{1,0:T(8,128)(2,1)S(1)}, u32[]{:S(2)}) copy-start(bf16[64,4096]{1,0:T(8,128)(2,1)S(1)} %collective-permute-done.2.refs_6_) | copy-start | bytes 1572868
  60.7 15.3 %collective-permute-start.3 = (bf16[64,4096]{1,0:T(8,128)(2,1)S(1)}, bf16[64,4096]{1,0:T(8,128)(2,1)S(1)}, u32[]{:S(2)}, u32[]{:S(2)}) collective-permute-start(bf16[64,4096]{1,0:T(8,128)(2,1)S(1)} %collective-permute-done.2.refs_6_), channel_id=1, source_target_pairs={{0,16},{1,49},{2,18},{3,51},{4,20},{5,53},{6,22},{7,55},{8,24},{9,... | collective-permute-start | bytes 1572872 | tf_op jit(solution)/shard_map/ppermute | solution.py:160
  74.3 10.4 %collective-permute-start.12 = (bf16[64,4096]{1,0:T(8,128)(2,1)S(1)}, bf16[64,4096]{1,0:T(8,128)(2,1)S(1)}, u32[]{:S(2)}, u32[]{:S(2)}) collective-permute-start(bf16[64,4096]{1,0:T(8,128)(2,1)S(1)} %pad_maximum_fusion.refs_11_), channel_id=1, source_target_pairs={{0,16},{1,49},{2,18},{3,51},{4,20},{5,53},{6,22},{7,55},{8,24},{9,... | collective-permute-start | bytes 1572872 | tf_op jit(solution)/shard_map/ppermute | solution.py:160
  76.9 13.5 %collective-permute-start.4 = (bf16[64,4096]{1,0:T(8,128)(2,1)S(1)}, bf16[64,4096]{1,0:T(8,128)(2,1)S(1)}, u32[]{:S(2)}, u32[]{:S(2)}) collective-permute-start(bf16[64,4096]{1,0:T(8,128)(2,1)S(1)} %collective-permute-done.refs_3_), channel_id=1, source_target_pairs={{0,16},{1,49},{2,18},{3,51},{4,20},{5,53},{6,22},{7,55},{8,24},{9,... | collective-permute-start | bytes 1572872 | tf_op jit(solution)/shard_map/ppermute | solution.py:160
  84.7 11.3 %collective-permute-start.13 = (bf16[64,4096]{1,0:T(8,128)(2,1)S(1)}, bf16[64,4096]{1,0:T(8,128)(2,1)}, u32[]{:S(2)}, u32[]{:S(2)}) collective-permute-start(bf16[64,4096]{1,0:T(8,128)(2,1)S(1)} %collective-permute-done.12.refs_13_), channel_id=1, source_target_pairs={{0,16},{1,49},{2,18},{3,51},{4,20},{5,53},{6,22},{7,55},{8,24},{9,... | collective-permute-start | bytes 1572872 | tf_op jit(solution)/shard_map/ppermute | solution.py:160
  90.4 11.3 %collective-permute-start.5 = (bf16[64,4096]{1,0:T(8,128)(2,1)S(1)}, bf16[64,4096]{1,0:T(8,128)(2,1)}, u32[]{:S(2)}, u32[]{:S(2)}) collective-permute-start(bf16[64,4096]{1,0:T(8,128)(2,1)S(1)} %collective-permute-done.4.refs_5_), channel_id=1, source_target_pairs={{0,16},{1,49},{2,18},{3,51},{4,20},{5,53},{6,22},{7,55},{8,24},{9,... | collective-permute-start | bytes 1572872 | tf_op jit(solution)/shard_map/ppermute | solution.py:160
  96.1 11.2 %collective-permute-start.14 = (bf16[64,4096]{1,0:T(8,128)(2,1)}, bf16[64,4096]{1,0:T(8,128)(2,1)}, u32[]{:S(2)}, u32[]{:S(2)}) collective-permute-start(bf16[64,4096]{1,0:T(8,128)(2,1)} %collective-permute-done.13.refs_15_), channel_id=1, source_target_pairs={{0,16},{1,49},{2,18},{3,51},{4,20},{5,53},{6,22},{7,55},{8,24},{9,... | collective-permute-start | bytes 1572872 | tf_op jit(solution)/shard_map/ppermute | solution.py:160
  101.7 11.2 %collective-permute-start.6 = (bf16[64,4096]{1,0:T(8,128)(2,1)}, bf16[64,4096]{1,0:T(8,128)(2,1)}, u32[]{:S(2)}, u32[]{:S(2)}) collective-permute-start(bf16[64,4096]{1,0:T(8,128)(2,1)} %collective-permute-done.5.refs_7_), channel_id=1, source_target_pairs={{0,16},{1,49},{2,18},{3,51},{4,20},{5,53},{6,22},{7,55},{8,24},{9,... | collective-permute-start | bytes 1572872 | tf_op jit(solution)/shard_map/ppermute | solution.py:160
  112.9 1.0 copy-start.3
  114.0 1.0 copy-start.6
  115.0 1.2 copy-start.9
  152.7 2.2 %copy-start.1 = (bf16[512,4096]{1,0:T(8,128)(2,1)S(1)}, bf16[512,4096]{1,0:T(8,128)(2,1)}, u32[]{:S(2)}) copy-start(bf16[512,4096]{1,0:T(8,128)(2,1)} %all-gather.3.cloned.1.call-done.refs_1_) | copy-start | bytes 12582916
  (15 other events, 14.0 us)
Sparse Core Ops, SparseCore 0:
  13.2 92.0 all-gather.4
  107.0 35.4 all-gather.2

commit v2 on v0

v2 whole, which is shorter than its diff:
```python
import jax
import jax.numpy as jnp
from jax import lax
from jax.experimental import pallas as pl
from jax.experimental.pallas import tpu as pltpu
from jax.sharding import PartitionSpec as P

NT = (((1,), (1,)), ((), ()))
LANES = 128
N_ROW, N_COL = 8, 16
PIECE = 64
VMEM = 60 << 20


def permutations():
    y_ring, z_ring = [], []
    for c in range(N_COL):
        way = 1 if c % 2 == 0 else -1
        y_ring.append((c, c // 8 * 8 + (c // 2 % 4 + way) % 4 * 2 + c % 2))
        for r in range(N_ROW):
            z_ring.append((r * N_COL + c, (r // 4 * 4 + (r % 4 + way) % 4) * N_COL + c))
    return {
        "y": ("col", y_ring),
        "z": (("row", "col"), z_ring),
        "x_lo": ("col", [(c, c ^ 8) for c in range(N_COL)]),
        "x_hi": ("row", [(r, r ^ 4) for r in range(N_ROW)]),
        "core": ("col", [(c, c ^ 1) for c in range(N_COL)]),
    }


PERMUTATIONS = permutations()


def send(kind, block, *earlier):
    axis, pairs = PERMUTATIONS[kind]
    return lax.ppermute(after(block, *earlier), axis, pairs)


def after(value, *earlier):
    return lax.optimization_barrier((value,) + earlier)[0] if earlier else value


def scale(three_index, occ_index, vir_index, occ_energy, vir_energy, frequency):
    rows, pairs = three_index.shape
    chunks = pairs // LANES

    def table(energy):
        padded = -(-energy.shape[0] // (8 * LANES)) * 8 * LANES
        return jnp.pad(energy, (0, padded - energy.shape[0])).reshape(-1, LANES)

    def kernel(freq, occ, vir, occ_table, vir_table, b, *outs):
        def look_up(table_ref, index):
            high, low = index >> 7, index & (LANES - 1)
            found = jnp.zeros(index.shape, jnp.float32)
            for k in range(table_ref.shape[0]):
                line = jnp.broadcast_to(table_ref[k : k + 1, :], index.shape)
                found = jnp.where(high == k, jnp.take_along_axis(line, low, axis=1), found)
            return found

        gap = look_up(vir_table, vir[...]) - look_up(occ_table, occ[...])
        denominator = -4.0 * gap / (gap * gap + freq[0] * freq[0])
        for k in range(chunks):
            at = slice(k * LANES, (k + 1) * LANES)
            scaled = (b[:, at].astype(jnp.float32) * denominator[k : k + 1, :]).astype(jnp.bfloat16)
            for h, out in enumerate(outs):
                out[:, at] = scaled[h * PIECE : (h + 1) * PIECE]

    vmem = pl.BlockSpec(memory_space=pltpu.VMEM)
    return pl.pallas_call(
        kernel,
        out_shape=[jax.ShapeDtypeStruct((PIECE, pairs), jnp.bfloat16)] * 2,
        in_specs=[pl.BlockSpec(memory_space=pltpu.SMEM)] + [vmem] * 5,
        out_specs=[vmem] * 2,
        compiler_params=pltpu.CompilerParams(vmem_limit_bytes=32 << 20),
    )(
        frequency,
        occ_index.reshape(chunks, LANES),
        vir_index.reshape(chunks, LANES),
        table(occ_energy),
        table(vir_energy),
        three_index,
    )


def multiply(a_parts, a_rows, j_groups, out):
    depth = a_parts[0].shape[1]
    pieces = [(p, t) for p, part in enumerate(a_parts) for t in range(part.shape[0] // PIECE)]
    tiles = [pieces[i : i + 8] for i in range(0, len(pieces), 8)]
    sizes = [len(g[1]) for g in j_groups]
    n_a, n_j, n_g = len(a_parts), sum(sizes), len(j_groups)
    width = 4 * LANES
    numbers = jnp.stack(list(a_rows) + [x for g in j_groups for x in g[2]] + [g[0] for g in j_groups]).astype(jnp.int32)
    has = out is not None

    def kernel(number, *refs):
        a_refs, j_refs = refs[:n_a], refs[n_a : n_a + n_j]
        o, j_all, a_buf, acc, j_sem, a_sem, o_sem = refs[-7:]
        j_loads = []
        for g in range(n_g):
            first = sum(sizes[:g])
            loads = []
            for j in range(first, first + sizes[g]):
                to = pl.multiple_of(number[len(pieces) + j], PIECE)
                n = j_refs[j].shape[0]
                loads.append(pltpu.make_async_copy(j_refs[j], j_all.at[g, pl.ds(to, n)], j_sem.at[j]))
            j_loads.append(loads)

        def a_load(t):
            return [
                pltpu.make_async_copy(
                    a_refs[p].at[pl.ds(s * PIECE, PIECE)], a_buf.at[t % 2, pl.ds(i * PIECE, PIECE)], a_sem.at[t % 2, i]
                )
                for i, (p, s) in enumerate(tiles[t])
            ]

        for c in j_loads[0] + a_load(0) + sum(j_loads[1:], []):
            c.start()
        pending = [[], []]
        step = 0
        for t, tile in enumerate(tiles):
            for c in a_load(t):
                c.wait()
            if t + 1 < len(tiles):
                for c in a_load(t + 1):
                    c.start()
            m = len(tile) * PIECE
            for g in range(n_g):
                if t == 0:
                    for c in j_loads[g]:
                        c.wait()
                slot = step % 2
                step += 1
                for c in pending[slot]:
                    c.wait()
                for w in range(2):
                    product = lax.dot_general(
                        a_buf[t % 2, :m], j_all[g, w * 256 : (w + 1) * 256, :], NT, preferred_element_type=jnp.float32
                    )
                    acc[slot, :m, 2 * w : 2 * w + 2, :] = product.reshape(m, 2, LANES)
                half = number[len(pieces) + n_j + g]
                pending[slot] = []
                for i in range(len(tile)):
                    to = pl.multiple_of(number[t * 8 + i], PIECE)
                    c = pltpu.make_async_copy(
                        acc.at[slot, pl.ds(i * PIECE, PIECE)], o.at[pl.ds(to, PIECE), half], o_sem.at[slot, i]
                    )
                    c.start()
                    pending[slot].append(c)
        for p in pending:
            for c in p:
                c.wait()

    hbm = pl.BlockSpec(memory_space=pl.ANY)
    return pl.pallas_call(
        kernel,
        out_shape=jax.ShapeDtypeStruct((N_COL * LANES, 2, 4, LANES), jnp.float32),
        in_specs=[pl.BlockSpec(memory_space=pltpu.SMEM)] + [hbm] * (n_a + n_j + has),
        out_specs=hbm,
        input_output_aliases={1 + n_a + n_j: 0} if has else {},
        scratch_shapes=[
            pltpu.VMEM((n_g, width, depth), jnp.bfloat16),
            pltpu.VMEM((2, 8 * PIECE, depth), jnp.bfloat16),
            pltpu.VMEM((2, 8 * PIECE, 4, LANES), jnp.float32),
            pltpu.SemaphoreType.DMA((n_j,)),
            pltpu.SemaphoreType.DMA((2, 8)),
            pltpu.SemaphoreType.DMA((2, 8)),
        ],
        compiler_params=pltpu.CompilerParams(vmem_limit_bytes=VMEM),
        cost_estimate=pl.CostEstimate(
            flops=2 * len(pieces) * PIECE * n_g * width * depth, bytes_accessed=16 << 20, transcendentals=0
        ),
    )(numbers, *a_parts, *[x for g in j_groups for x in g[1]], *([out] if has else []))


def shards(three_index, occ_index, vir_index, occ_energy, vir_energy, frequency):
    raw = [three_index[:PIECE], three_index[PIECE:]]
    scaled = scale(three_index, occ_index, vir_index, occ_energy, vir_energy, frequency)
    two = range(2)

    a_far, j_far = [send("x_lo", scaled[0])], [send("x_hi", raw[0])]
    a_far.append(send("x_lo", scaled[1], a_far[0]))
    j_far.append(send("x_hi", raw[1], j_far[0]))
    a = [[scaled[h]] for h in two]
    j = [[raw[h]] for h in two]
    for _ in range(3):
        for h in two:
            a[h].append(send("y", a[h][-1]))
            j[h].append(send("z", j[h][-1]))
    near_done = [a[h][3] for h in two] + [j[h][3] for h in two]
    an, jn = [], []
    for h in two:
        x, v, *_ = lax.optimization_barrier((a_far[h], j_far[h], a[h][3], j[h][3]))
        an.append([x])
        jn.append([v])
    for _ in range(3):
        for h in two:
            an[h].append(send("y", an[h][-1]))
            jn[h].append(send("z", jn[h][-1]))

    flat = lambda blocks, steps: [blocks[h][i] for i in steps for h in two]
    a_near, an_most, an_last = flat(a, range(4)), flat(an, range(3)), flat(an, [3])
    near_other = send("core", jnp.concatenate(a_near, 0), *near_done)
    most_other = send("core", jnp.concatenate(an_most, 0), jn[0][2], jn[1][2])
    last_other = send("core", jnp.concatenate(an_last, 0), jn[0][3], jn[1][3])

    row, col = lax.axis_index("row"), lax.axis_index("col")
    x_hi, z, x_lo, y, core = row // 4, row % 4, col // 8, col // 2 % 4, col % 2
    way = 1 - 2 * core

    def rows(x, other, steps):
        k, w = (1 - core, -way) if other else (core, way)
        return [((x * 4 + (y - i * w) % 4) * 2 + k) * LANES + h * PIECE for i in steps for h in two]

    places = [(z - i * way) % 4 * LANES + h * PIECE for i in range(4) for h in two]
    j_near = (x_hi, flat(j, range(4)), places)
    j_rest = (1 - x_hi, flat(jn, range(4)), places)
    near = (a_near + [near_other], rows(x_lo, 0, range(4)) + rows(x_lo, 1, range(4)))
    most = (an_most + [most_other], rows(1 - x_lo, 0, range(3)) + rows(1 - x_lo, 1, range(3)))
    last = (an_last + [last_other], rows(1 - x_lo, 0, [3]) + rows(1 - x_lo, 1, [3]))
    out = multiply(*near, [j_near], None)
    out = multiply(*most, [j_near], out)
    out = multiply(near[0] + most[0], near[1] + most[1], [j_rest], out)
    out = multiply(*last, [j_near, j_rest], out)
    return out.reshape(N_COL * LANES, N_ROW, 1, LANES)


def solution(mesh):
    placed = (P(("row", "col"), None), P(), P(), P(), P(), P())
    return jax.shard_map(
        shards, mesh=mesh, in_specs=placed, out_specs=P("row", None, "col", None), check_vma=False
    )
```

time: 277 us -> 157 us (0.57)
  waiting for transfers between devices: 163 us -> 39.7 us
  Pallas kernels: 0 us -> 43.6 us
  local copies, waits for them, and re-layouts: 64.4 us -> 21.6 us
  starting transfers between devices: 6.95 us -> 48.4 us
  matrix products: 24.2 us -> 0 us
  between operations: 14.1 us -> 1.41 us
    all_gather x2 -> x0, waiting for transfers between devices: 163 us -> none  [the longest x1 99.6 us: shards(): lax.all_gather(panel, 'col', axis=1, tiled=True)]
    ppermute x0 -> x31, starting transfers between devices: none -> 48.4 us  [send(): return lax.ppermute(after(block, *earlier), axis, pairs)]
    pallas_call x0 -> x5, Pallas kernels: none -> 43.6 us  [the longest x4 42.8 us: multiply(): pl.pallas_call(kernel, out_shape=jax.ShapeDtypeStruct((N_COL * LANES, 2,...]
    ppermute x0 -> x31, waiting for transfers between devices: none -> 39.7 us  [send(): return lax.ppermute(after(block, *earlier), axis, pairs)]
    gather x2 -> x0, local copies, waits for them, and re-layouts: 39.7 us -> none  [shards(): gap = jnp.take(vir_energy, vir_index) - jnp.take(occ_energy, occ_index)]
    dot_general x1 -> x0, matrix products: 24.2 us -> none  [shards(): lax.dot_general(lax.all_gather(panel, 'col', axis=1, tiled=True), column_...]
    reshape x1 -> x2, local copies, waits for them, and re-layouts: 20.5 us -> 1.41 us  [table(): return jnp.pad(energy, (0, padded - energy.shape[0])).reshape(-1, LANES)]
    unnamed x9 -> x72, local copies, waits for them, and re-layouts: 2.28 us -> 15.7 us
  transfers between devices with their start and end apart: 3 -> 31, of which waited for: 2 -> 14; matrix products, arithmetic and copies ran while one was open for 17% -> 11% of each run, Pallas kernels for 0% -> 22%
where the time goes in v2:
time: 157 us
  starting transfers between devices  48.4 us (31%)
  Pallas kernels  43.6 us (28%)
  waiting for transfers between devices  39.7 us (25%)
  local copies, waits for them, and re-layouts  21.6 us (14%)
  other arithmetic  2.27 us (1%)
    ppermute x31, starting transfers between devices, send(): return lax.ppermute(after(block, *earlier), axis, pairs)  48.4 us
    pallas_call x4, Pallas kernels, multiply(): pl.pallas_call(kernel, out_shape=jax.ShapeDtypeStruct((N_COL * LANES, 2,...  42.8 us
    ppermute x31, waiting for transfers between devices, send(): return lax.ppermute(after(block, *earlier), axis, pairs)  39.7 us
    unnamed x72, local copies, waits for them, and re-layouts  15.7 us
  transfers between devices with their start and end apart: 31, of which 14 were waited for; matrix products, arithmetic and copies ran while one was open for 11% of the time, Pallas kernels for 22%

profile of v2, /device:TPU:1, one launch (start us, length us, event | category | flops | bytes accessed | tf_op | source)
XLA Modules:
  0.0 157.0 jit_solution(296455660239181531)
XLA Ops:
  5.6 3.6 %collective-permute-start.2 = (bf16[64,4096]{1,0:T(8,128)(2,1)S(1)}, bf16[64,4096]{1,0:T(8,128)(2,1)S(1)}, u32[]{:S(2)}, u32[]{:S(2)}) collective-permute-start(bf16[64,4096]{1,0:T(8,128)(2,1)S(1)} %get-tuple-element.16.refs_0_), channel_id=1, source_target_pairs={{0,2},{1,7},{2,4},{3,1},{4,6},{5,3},{6,0},{7,5},{8,10},{9,15},{10,... | collective-permute-start | bytes 1572872 | tf_op jit(solution)/shard_map/ppermute | solution.py:36
  10.5 3.8 %collective-permute-start.5 = (bf16[64,4096]{1,0:T(8,128)(2,1)S(1)}, bf16[64,4096]{1,0:T(8,128)(2,1)S(1)}, u32[]{:S(2)}, u32[]{:S(2)}) collective-permute-start(bf16[64,4096]{1,0:T(8,128)(2,1)S(1)} %get-tuple-element.28.refs_9_.refs_7_.refs_3_), channel_id=1, source_target_pairs={{0,16},{16,32},{32,48},{48,0},{64,80},{80,96},{96,112},{112,64},{1... | collective-permute-start | bytes 1572872 | tf_op jit(solution)/shard_map/ppermute | solution.py:36
  14.4 2.5 %collective-permute-start.1 = (bf16[64,4096]{1,0:T(8,128)(2,1)S(1)}, bf16[64,4096]{1,0:T(8,128)(2,1)S(1)}, u32[]{:S(2)}, u32[]{:S(2)}) collective-permute-start(bf16[64,4096]{1,0:T(8,128)(2,1)S(1)} %get-tuple-element.28.refs_9_.refs_7_.refs_3_), channel_id=1, source_target_pairs={{0,64},{16,80},{32,96},{48,112},{64,0},{80,16},{96,32},{112,48},{1... | collective-permute-start | bytes 1572872 | tf_op jit(solution)/shard_map/ppermute | solution.py:36
  19.1 6.0 %collective-permute-done.13.refs_3_ = bf16[64,4096]{1,0:T(8,128)(2,1)S(1)} collective-permute-done((bf16[64,4096]{1,0:T(8,128)(2,1)S(1)}, bf16[64,4096]{1,0:T(8,128)(2,1)S(1)}, u32[]{:S(2)}, u32[]{:S(2)}) %collective-permute-start.13) | collective-permute-done | bytes 524320 | tf_op jit(solution)/shard_map/ppermute | solution.py:36
  29.6 6.9 %collective-permute-done.1.refs_16_.refs_11_ = bf16[64,4096]{1,0:T(8,128)(2,1)S(1)} collective-permute-done((bf16[64,4096]{1,0:T(8,128)(2,1)S(1)}, bf16[64,4096]{1,0:T(8,128)(2,1)S(1)}, u32[]{:S(2)}, u32[]{:S(2)}) %collective-permute-start.1) | collective-permute-done | bytes 524320 | tf_op jit(solution)/shard_map/ppermute | solution.py:36
  36.6 3.8 %collective-permute-start.17 = (bf16[64,4096]{1,0:T(8,128)(2,1)S(1)}, bf16[64,4096]{1,0:T(8,128)(2,1)S(1)}, u32[]{:S(2)}, u32[]{:S(2)}) collective-permute-start(bf16[64,4096]{1,0:T(8,128)(2,1)S(1)} %collective-permute-done.16.refs_12_.refs_10_.refs_6_), channel_id=1, source_target_pairs={{0,16},{16,32},{32,48},{48,0},{64,80},{80,96},{96,112},{112,64},{1... | collective-permute-start | bytes 1572872 | tf_op jit(solution)/shard_map/ppermute | solution.py:36
  43.7 2.8 %collective-permute-done.17.refs_14_.refs_12_.refs_8_ = bf16[64,4096]{1,0:T(8,128)(2,1)S(1)} collective-permute-done((bf16[64,4096]{1,0:T(8,128)(2,1)S(1)}, bf16[64,4096]{1,0:T(8,128)(2,1)S(1)}, u32[]{:S(2)}, u32[]{:S(2)}) %collective-permute-start.17) | collective-permute-done | bytes 524320 | tf_op jit(solution)/shard_map/ppermute | solution.py:36
  46.5 2.2 %collective-permute-done.4.refs_6_ = bf16[64,4096]{1,0:T(8,128)(2,1)S(1)} collective-permute-done((bf16[64,4096]{1,0:T(8,128)(2,1)S(1)}, bf16[64,4096]{1,0:T(8,128)(2,1)S(1)}, u32[]{:S(2)}, u32[]{:S(2)}) %collective-permute-start.4) | collective-permute-done | bytes 524320 | tf_op jit(solution)/shard_map/ppermute | solution.py:36
  62.6 2.8 %collective-permute-start.25 = (bf16[64,4096]{1,0:T(8,128)(2,1)S(1)}, bf16[64,4096]{1,0:T(8,128)(2,1)S(1)}, u32[]{:S(2)}, u32[]{:S(2)}) collective-permute-start(bf16[64,4096]{1,0:T(8,128)(2,1)S(1)} %collective-permute-done.12.refs_17_.refs_12_), channel_id=1, source_target_pairs={{0,16},{16,32},{32,48},{48,0},{64,80},{80,96},{96,112},{112,64},{1... | collective-permute-start | bytes 1572872 | tf_op jit(solution)/shard_map/ppermute | solution.py:36
  66.5 2.6 %collective-permute-done.19.refs_3_.refs_12_ = bf16[64,4096]{1,0:T(8,128)(2,1)S(1)} collective-permute-done((bf16[64,4096]{1,0:T(8,128)(2,1)S(1)}, bf16[64,4096]{1,0:T(8,128)(2,1)S(1)}, u32[]{:S(2)}, u32[]{:S(2)}) %collective-permute-start.19) | collective-permute-done | bytes 524320 | tf_op jit(solution)/shard_map/ppermute | solution.py:36
  69.1 2.2 %collective-permute-start.20 = (bf16[64,4096]{1,0:T(8,128)(2,1)S(1)}, bf16[64,4096]{1,0:T(8,128)(2,1)S(1)}, u32[]{:S(2)}, u32[]{:S(2)}) collective-permute-start(bf16[64,4096]{1,0:T(8,128)(2,1)S(1)} %collective-permute-done.19.refs_3_.refs_12_), channel_id=1, source_target_pairs={{0,2},{1,7},{2,4},{3,1},{4,6},{5,3},{6,0},{7,5},{8,10},{9,15},{10,... | collective-permute-start | bytes 1572872 | tf_op jit(solution)/shard_map/ppermute | solution.py:36
  72.2 2.8 %collective-permute-start.26 = (bf16[64,4096]{1,0:T(8,128)(2,1)S(1)}, bf16[64,4096]{1,0:T(8,128)(2,1)}, u32[]{:S(2)}, u32[]{:S(2)}) collective-permute-start(bf16[64,4096]{1,0:T(8,128)(2,1)S(1)} %collective-permute-done.25.refs_19_.refs_14_), channel_id=1, source_target_pairs={{0,16},{16,32},{32,48},{48,0},{64,80},{80,96},{96,112},{112,64},{1... | collective-permute-start | bytes 1572872 | tf_op jit(solution)/shard_map/ppermute | solution.py:36
  75.0 2.2 %collective-permute-done.22.refs_18_.refs_13_ = bf16[64,4096]{1,0:T(8,128)(2,1)S(1)} collective-permute-done((bf16[64,4096]{1,0:T(8,128)(2,1)S(1)}, bf16[64,4096]{1,0:T(8,128)(2,1)S(1)}, u32[]{:S(2)}, u32[]{:S(2)}) %collective-permute-start.22) | collective-permute-done | bytes 524320 | tf_op jit(solution)/shard_map/ppermute | solution.py:36
  77.2 3.5 %collective-permute-start.23 = (bf16[64,4096]{1,0:T(8,128)(2,1)S(1)}, bf16[64,4096]{1,0:T(8,128)(2,1)}, u32[]{:S(2)}, u32[]{:S(2)}) collective-permute-start(bf16[64,4096]{1,0:T(8,128)(2,1)S(1)} %collective-permute-done.22.refs_18_.refs_13_), channel_id=1, source_target_pairs={{0,16},{16,32},{32,48},{48,0},{64,80},{80,96},{96,112},{112,64},{1... | collective-permute-start | bytes 1572872 | tf_op jit(solution)/shard_map/ppermute | solution.py:36
  83.5 4.9 %collective-permute-done.23.refs_20_.refs_15_ = bf16[64,4096]{1,0:T(8,128)(2,1)} collective-permute-done((bf16[64,4096]{1,0:T(8,128)(2,1)S(1)}, bf16[64,4096]{1,0:T(8,128)(2,1)}, u32[]{:S(2)}, u32[]{:S(2)}) %collective-permute-start.23) | collective-permute-done | bytes 524320 | tf_op jit(solution)/shard_map/ppermute | solution.py:36
  88.5 2.6 %collective-permute-start.30 = (bf16[384,4096]{1,0:T(8,128)(2,1)}, bf16[384,4096]{1,0:T(8,128)(2,1)S(1)}, u32[]{:S(2)}, u32[]{:S(2)}) collective-permute-start(bf16[384,4096]{1,0:T(8,128)(2,1)} %constant_dynamic-update-slice_fusion.8), channel_id=1, source_target_pairs={{0,1},{1,0},{2,3},{3,2},{4,5},{5,4},{6,7},{7,6},{8,9},{9,8},{10,11... | collective-permute-start | bytes 9437192 | tf_op jit(solution)/shard_map/ppermute | solution.py:36
  91.1 2.9 %collective-permute-start.21 = (bf16[64,4096]{1,0:T(8,128)(2,1)S(1)}, bf16[64,4096]{1,0:T(8,128)(2,1)S(1)}, u32[]{:S(2)}, u32[]{:S(2)}) collective-permute-start(bf16[64,4096]{1,0:T(8,128)(2,1)S(1)} %collective-permute-done.20.refs_5_.refs_14_), channel_id=1, source_target_pairs={{0,2},{1,7},{2,4},{3,1},{4,6},{5,3},{6,0},{7,5},{8,10},{9,15},{10,... | collective-permute-start | bytes 1572872 | tf_op jit(solution)/shard_map/ppermute | solution.py:36
  95.8 4.3 %collective-permute-done.21.refs_1_ = bf16[64,4096]{1,0:T(8,128)(2,1)S(1)} collective-permute-done((bf16[64,4096]{1,0:T(8,128)(2,1)S(1)}, bf16[64,4096]{1,0:T(8,128)(2,1)S(1)}, u32[]{:S(2)}, u32[]{:S(2)}) %collective-permute-start.21) | collective-permute-done | bytes 524320 | tf_op jit(solution)/shard_map/ppermute | solution.py:36
  105.8 2.3 %pad_maximum_fusion = bf16[128,4096]{1,0:T(8,128)(2,1)} fusion(bf16[64,4096]{1,0:T(8,128)(2,1)} %copy-done.29, bf16[64,4096]{1,0:T(8,128)(2,1)} %collective-permute-done.10.refs_0_), kind=kLoop, calls=%fused_computation | loop fusion | flops 2097152 | bytes 2097152 | tf_op jit(solution)/shard_map/concatenate | solution.py:204
  108.8 3.5 %collective-permute-start.28 = (bf16[128,4096]{1,0:T(8,128)(2,1)}, bf16[128,4096]{1,0:T(8,128)(2,1)}, u32[]{:S(2)}, u32[]{:S(2)}) collective-permute-start(bf16[128,4096]{1,0:T(8,128)(2,1)} %pad_maximum_fusion), channel_id=1, source_target_pairs={{0,1},{1,0},{2,3},{3,2},{4,5},{5,4},{6,7},{7,6},{8,9},{9,8},{10,11... | collective-permute-start | bytes 3145736 | tf_op jit(solution)/shard_map/ppermute | solution.py:36
  112.3 10.6 %shard_map.65.refs_15_ = f32[2048,2,4,128]{3,2,1,0:T(4,128)} custom-call(s32[25]{0:T(128)} %stack.246.number, bf16[64,4096]{1,0:T(8,128)(2,1)} %copy-done, bf16[64,4096]{1,0:T(8,128)(2,1)} %copy-done.1, bf16[64,4096]{1,0:T(8,128)(2,1)} %copy-done.8, bf16[64,4096]{1,0:T(8,128)(2,1)} %copy-done.10, bf16[64,4096]{1,0:T(8,128)(2,1)} %copy-done.11, ...), custom_call_target="tpu_custom_call" | custom-call | flops 4294967296 | bytes 16777216 | tf_op jit(solution)/shard_map/pallas_call | solution.py:154
  124.5 9.2 %shard_map.66.refs_24_ = f32[2048,2,4,128]{3,2,1,0:T(4,128)} custom-call(s32[21]{0:T(128)} %stack.245.number, bf16[64,4096]{1,0:T(8,128)(2,1)} %copy-done.9, bf16[64,4096]{1,0:T(8,128)(2,1)} %copy-done.13, bf16[64,4096]{1,0:T(8,128)(2,1)} %copy-done.16, bf16[64,4096]{1,0:T(8,128)(2,1)} %copy-done.17, ...), custom_call_target="tpu_custom_call", output_to_operand_aliasing={{}: (16, {})} | custom-call | flops 3221225472 | bytes 16777216 | tf_op jit(solution)/shard_map/pallas_call | solution.py:154
  133.7 14.7 %shard_map.67.refs_19_ = f32[2048,2,4,128]{3,2,1,0:T(4,128)} custom-call(s32[37]{0:T(128)} %stack.244.number, bf16[64,4096]{1,0:T(8,128)(2,1)} %copy-done, bf16[64,4096]{1,0:T(8,128)(2,1)} %copy-done.1, bf16[64,4096]{1,0:T(8,128)(2,1)} %copy-done.8, bf16[64,4096]{1,0:T(8,128)(2,1)} %copy-done.10, ...), custom_call_target="tpu_custom_call", output_to_operand_aliasing={{}: (25, {})} | custom-call | flops 7516192768 | bytes 16777216 | tf_op jit(solution)/shard_map/pallas_call | solution.py:154
  148.4 8.4 %shard_map.68 = f32[2048,2,4,128]{3,2,1,0:T(4,128)} custom-call(s32[22]{0:T(128)} %stack.106.number, bf16[64,4096]{1,0:T(8,128)(2,1)} %collective-permute-done.10.refs_0_, bf16[64,4096]{1,0:T(8,128)(2,1)} %copy-done.29, bf16[128,4096]{1,0:T(8,128)(2,1)} %collective-permute-done.28.refs_2_, ...), custom_call_target="tpu_custom_call", output_to_operand_aliasing={{}: (20, {})} | custom-call | flops 2147483648 | bytes 16777216 | tf_op jit(solution)/shard_map/pallas_call | solution.py:154
  (125 shorter events, 44.3 us)
Async XLA Ops:
  5.6 13.4 %collective-permute-start.2 = (bf16[64,4096]{1,0:T(8,128)(2,1)S(1)}, bf16[64,4096]{1,0:T(8,128)(2,1)S(1)}, u32[]{:S(2)}, u32[]{:S(2)}) collective-permute-start(bf16[64,4096]{1,0:T(8,128)(2,1)S(1)} %get-tuple-element.16.refs_0_), channel_id=1, source_target_pairs={{0,2},{1,7},{2,4},{3,1},{4,6},{5,3},{6,0},{7,5},{8,10},{9,15},{10,... | collective-permute-start | bytes 1572872 | tf_op jit(solution)/shard_map/ppermute | solution.py:36
  9.2 19.5 %collective-permute-start = (bf16[64,4096]{1,0:T(8,128)(2,1)S(1)}, bf16[64,4096]{1,0:T(8,128)(2,1)S(1)}, u32[]{:S(2)}, u32[]{:S(2)}) collective-permute-start(bf16[64,4096]{1,0:T(8,128)(2,1)S(1)} %get-tuple-element.16.refs_0_), channel_id=1, source_target_pairs={{0,8},{1,9},{2,10},{3,11},{4,12},{5,13},{6,14},{7,15},{8,0},{9,1},... | collective-permute-start | bytes 1572872 | tf_op jit(solution)/shard_map/ppermute | solution.py:36
  10.5 16.3 %collective-permute-start.5 = (bf16[64,4096]{1,0:T(8,128)(2,1)S(1)}, bf16[64,4096]{1,0:T(8,128)(2,1)S(1)}, u32[]{:S(2)}, u32[]{:S(2)}) collective-permute-start(bf16[64,4096]{1,0:T(8,128)(2,1)S(1)} %get-tuple-element.28.refs_9_.refs_7_.refs_3_), channel_id=1, source_target_pairs={{0,16},{16,32},{32,48},{48,0},{64,80},{80,96},{96,112},{112,64},{1... | collective-permute-start | bytes 1572872 | tf_op jit(solution)/shard_map/ppermute | solution.py:36
  14.4 22.2 %collective-permute-start.1 = (bf16[64,4096]{1,0:T(8,128)(2,1)S(1)}, bf16[64,4096]{1,0:T(8,128)(2,1)S(1)}, u32[]{:S(2)}, u32[]{:S(2)}) collective-permute-start(bf16[64,4096]{1,0:T(8,128)(2,1)S(1)} %get-tuple-element.28.refs_9_.refs_7_.refs_3_), channel_id=1, source_target_pairs={{0,64},{16,80},{32,96},{48,112},{64,0},{80,16},{96,32},{112,48},{1... | collective-permute-start | bytes 1572872 | tf_op jit(solution)/shard_map/ppermute | solution.py:36
  18.9 17.6 %collective-permute-start.16 = (bf16[64,4096]{1,0:T(8,128)(2,1)S(1)}, bf16[64,4096]{1,0:T(8,128)(2,1)S(1)}, u32[]{:S(2)}, u32[]{:S(2)}) collective-permute-start(bf16[64,4096]{1,0:T(8,128)(2,1)S(1)} %get-tuple-element.20.refs_10_.refs_8_.refs_4_), channel_id=1, source_target_pairs={{0,16},{16,32},{32,48},{48,0},{64,80},{80,96},{96,112},{112,64},{1... | collective-permute-start | bytes 1572872 | tf_op jit(solution)/shard_map/ppermute | solution.py:36
  25.1 15.2 %collective-permute-start.3 = (bf16[64,4096]{1,0:T(8,128)(2,1)S(1)}, bf16[64,4096]{1,0:T(8,128)(2,1)S(1)}, u32[]{:S(2)}, u32[]{:S(2)}) collective-permute-start(bf16[64,4096]{1,0:T(8,128)(2,1)S(1)} %collective-permute-done.2.refs_2_), channel_id=1, source_target_pairs={{0,2},{1,7},{2,4},{3,1},{4,6},{5,3},{6,0},{7,5},{8,10},{9,15},{10,... | collective-permute-start | bytes 1572872 | tf_op jit(solution)/shard_map/ppermute | solution.py:36
  26.8 13.6 %collective-permute-start.6 = (bf16[64,4096]{1,0:T(8,128)(2,1)S(1)}, bf16[64,4096]{1,0:T(8,128)(2,1)S(1)}, u32[]{:S(2)}, u32[]{:S(2)}) collective-permute-start(bf16[64,4096]{1,0:T(8,128)(2,1)S(1)} %collective-permute-done.5.refs_11_.refs_9_.refs_5_), channel_id=1, source_target_pairs={{0,16},{16,32},{32,48},{48,0},{64,80},{80,96},{96,112},{112,64},{1... | collective-permute-start | bytes 1572872 | tf_op jit(solution)/shard_map/ppermute | solution.py:36
  28.7 12.9 %collective-permute-start.14 = (bf16[64,4096]{1,0:T(8,128)(2,1)S(1)}, bf16[64,4096]{1,0:T(8,128)(2,1)S(1)}, u32[]{:S(2)}, u32[]{:S(2)}) collective-permute-start(bf16[64,4096]{1,0:T(8,128)(2,1)S(1)} %collective-permute-done.13.refs_3_), channel_id=1, source_target_pairs={{0,2},{1,7},{2,4},{3,1},{4,6},{5,3},{6,0},{7,5},{8,10},{9,15},{10,... | collective-permute-start | bytes 1572872 | tf_op jit(solution)/shard_map/ppermute | solution.py:36
  36.5 23.3 %collective-permute-start.11 = (bf16[64,4096]{1,0:T(8,128)(2,1)S(1)}, bf16[64,4096]{1,0:T(8,128)(2,1)S(1)}, u32[]{:S(2)}, u32[]{:S(2)}) collective-permute-start(bf16[64,4096]{1,0:T(8,128)(2,1)S(1)} %get-tuple-element.19.refs_1_), channel_id=1, source_target_pairs={{0,8},{1,9},{2,10},{3,11},{4,12},{5,13},{6,14},{7,15},{8,0},{9,1},... | collective-permute-start | bytes 1572872 | tf_op jit(solution)/shard_map/ppermute | solution.py:36
  36.6 10.0 %collective-permute-start.17 = (bf16[64,4096]{1,0:T(8,128)(2,1)S(1)}, bf16[64,4096]{1,0:T(8,128)(2,1)S(1)}, u32[]{:S(2)}, u32[]{:S(2)}) collective-permute-start(bf16[64,4096]{1,0:T(8,128)(2,1)S(1)} %collective-permute-done.16.refs_12_.refs_10_.refs_6_), channel_id=1, source_target_pairs={{0,16},{16,32},{32,48},{48,0},{64,80},{80,96},{96,112},{112,64},{1... | collective-permute-start | bytes 1572872 | tf_op jit(solution)/shard_map/ppermute | solution.py:36
  40.4 11.7 %collective-permute-start.7 = (bf16[64,4096]{1,0:T(8,128)(2,1)S(1)}, bf16[64,4096]{1,0:T(8,128)(2,1)S(1)}, u32[]{:S(2)}, u32[]{:S(2)}) collective-permute-start(bf16[64,4096]{1,0:T(8,128)(2,1)S(1)} %collective-permute-done.6.refs_13_.refs_11_.refs_7_), channel_id=1, source_target_pairs={{0,16},{16,32},{32,48},{48,0},{64,80},{80,96},{96,112},{112,64},{1... | collective-permute-start | bytes 1572872 | tf_op jit(solution)/shard_map/ppermute | solution.py:36
  41.5 19.3 %collective-permute-start.12 = (bf16[64,4096]{1,0:T(8,128)(2,1)S(1)}, bf16[64,4096]{1,0:T(8,128)(2,1)S(1)}, u32[]{:S(2)}, u32[]{:S(2)}) collective-permute-start(bf16[64,4096]{1,0:T(8,128)(2,1)S(1)} %get-tuple-element.20.refs_10_.refs_8_.refs_4_), channel_id=1, source_target_pairs={{0,64},{16,80},{32,96},{48,112},{64,0},{80,16},{96,32},{112,48},{1... | collective-permute-start | bytes 1572872 | tf_op jit(solution)/shard_map/ppermute | solution.py:36
  53.0 12.6 %collective-permute-start.8 = (bf16[64,4096]{1,0:T(8,128)(2,1)S(1)}, bf16[64,4096]{1,0:T(8,128)(2,1)S(1)}, u32[]{:S(2)}, u32[]{:S(2)}) collective-permute-start(bf16[64,4096]{1,0:T(8,128)(2,1)S(1)} %collective-permute-done.refs_0_.refs_9_), channel_id=1, source_target_pairs={{0,2},{1,7},{2,4},{3,1},{4,6},{5,3},{6,0},{7,5},{8,10},{9,15},{10,... | collective-permute-start | bytes 1572872 | tf_op jit(solution)/shard_map/ppermute | solution.py:36
  57.7 54.6 %collective-permute-start.29 = (bf16[512,4096]{1,0:T(8,128)(2,1)}, bf16[512,4096]{1,0:T(8,128)(2,1)}, u32[]{:S(2)}, u32[]{:S(2)}) collective-permute-start(bf16[512,4096]{1,0:T(8,128)(2,1)} %constant_dynamic-update-slice_fusion), channel_id=1, source_target_pairs={{0,1},{1,0},{2,3},{3,2},{4,5},{5,4},{6,7},{7,6},{8,9},{9,8},{10,11... | collective-permute-start | bytes 12582920 | tf_op jit(solution)/shard_map/ppermute | solution.py:36
  62.6 9.6 %collective-permute-start.25 = (bf16[64,4096]{1,0:T(8,128)(2,1)S(1)}, bf16[64,4096]{1,0:T(8,128)(2,1)S(1)}, u32[]{:S(2)}, u32[]{:S(2)}) collective-permute-start(bf16[64,4096]{1,0:T(8,128)(2,1)S(1)} %collective-permute-done.12.refs_17_.refs_12_), channel_id=1, source_target_pairs={{0,16},{16,32},{32,48},{48,0},{64,80},{80,96},{96,112},{112,64},{1... | collective-permute-start | bytes 1572872 | tf_op jit(solution)/shard_map/ppermute | solution.py:36
  65.5 11.7 %collective-permute-start.22 = (bf16[64,4096]{1,0:T(8,128)(2,1)S(1)}, bf16[64,4096]{1,0:T(8,128)(2,1)S(1)}, u32[]{:S(2)}, u32[]{:S(2)}) collective-permute-start(bf16[64,4096]{1,0:T(8,128)(2,1)S(1)} %collective-permute-done.1.refs_16_.refs_11_), channel_id=1, source_target_pairs={{0,16},{16,32},{32,48},{48,0},{64,80},{80,96},{96,112},{112,64},{1... | collective-permute-start | bytes 1572872 | tf_op jit(solution)/shard_map/ppermute | solution.py:36
  65.6 15.1 %collective-permute-start.9 = (bf16[64,4096]{1,0:T(8,128)(2,1)S(1)}, bf16[64,4096]{1,0:T(8,128)(2,1)}, u32[]{:S(2)}, u32[]{:S(2)}) collective-permute-start(bf16[64,4096]{1,0:T(8,128)(2,1)S(1)} %collective-permute-done.8.refs_2_.refs_11_), channel_id=1, source_target_pairs={{0,2},{1,7},{2,4},{3,1},{4,6},{5,3},{6,0},{7,5},{8,10},{9,15},{10,... | collective-permute-start | bytes 1572872 | tf_op jit(solution)/shard_map/ppermute | solution.py:36
  69.1 13.5 %collective-permute-start.20 = (bf16[64,4096]{1,0:T(8,128)(2,1)S(1)}, bf16[64,4096]{1,0:T(8,128)(2,1)S(1)}, u32[]{:S(2)}, u32[]{:S(2)}) collective-permute-start(bf16[64,4096]{1,0:T(8,128)(2,1)S(1)} %collective-permute-done.19.refs_3_.refs_12_), channel_id=1, source_target_pairs={{0,2},{1,7},{2,4},{3,1},{4,6},{5,3},{6,0},{7,5},{8,10},{9,15},{10,... | collective-permute-start | bytes 1572872 | tf_op jit(solution)/shard_map/ppermute | solution.py:36
  72.2 11.3 %collective-permute-start.26 = (bf16[64,4096]{1,0:T(8,128)(2,1)S(1)}, bf16[64,4096]{1,0:T(8,128)(2,1)}, u32[]{:S(2)}, u32[]{:S(2)}) collective-permute-start(bf16[64,4096]{1,0:T(8,128)(2,1)S(1)} %collective-permute-done.25.refs_19_.refs_14_), channel_id=1, source_target_pairs={{0,16},{16,32},{32,48},{48,0},{64,80},{80,96},{96,112},{112,64},{1... | collective-permute-start | bytes 1572872 | tf_op jit(solution)/shard_map/ppermute | solution.py:36
  77.2 11.2 %collective-permute-start.23 = (bf16[64,4096]{1,0:T(8,128)(2,1)S(1)}, bf16[64,4096]{1,0:T(8,128)(2,1)}, u32[]{:S(2)}, u32[]{:S(2)}) collective-permute-start(bf16[64,4096]{1,0:T(8,128)(2,1)S(1)} %collective-permute-done.22.refs_18_.refs_13_), channel_id=1, source_target_pairs={{0,16},{16,32},{32,48},{48,0},{64,80},{80,96},{96,112},{112,64},{1... | collective-permute-start | bytes 1572872 | tf_op jit(solution)/shard_map/ppermute | solution.py:36
  88.5 34.4 %collective-permute-start.30 = (bf16[384,4096]{1,0:T(8,128)(2,1)}, bf16[384,4096]{1,0:T(8,128)(2,1)S(1)}, u32[]{:S(2)}, u32[]{:S(2)}) collective-permute-start(bf16[384,4096]{1,0:T(8,128)(2,1)} %constant_dynamic-update-slice_fusion.8), channel_id=1, source_target_pairs={{0,1},{1,0},{2,3},{3,2},{4,5},{5,4},{6,7},{7,6},{8,9},{9,8},{10,11... | collective-permute-start | bytes 9437192 | tf_op jit(solution)/shard_map/ppermute | solution.py:36
  94.0 11.8 %collective-permute-start.10 = (bf16[64,4096]{1,0:T(8,128)(2,1)}, bf16[64,4096]{1,0:T(8,128)(2,1)}, u32[]{:S(2)}, u32[]{:S(2)}) collective-permute-start(bf16[64,4096]{1,0:T(8,128)(2,1)} %collective-permute-done.9.refs_4_.refs_13_), channel_id=1, source_target_pairs={{0,2},{1,7},{2,4},{3,1},{4,6},{5,3},{6,0},{7,5},{8,10},{9,15},{10,... | collective-permute-start | bytes 1572872 | tf_op jit(solution)/shard_map/ppermute | solution.py:36
  94.1 14.0 %collective-permute-start.27 = (bf16[64,4096]{1,0:T(8,128)(2,1)}, bf16[64,4096]{1,0:T(8,128)(2,1)}, u32[]{:S(2)}, u32[]{:S(2)}) collective-permute-start(bf16[64,4096]{1,0:T(8,128)(2,1)} %collective-permute-done.26.refs_21_.refs_16_), channel_id=1, source_target_pairs={{0,16},{16,32},{32,48},{48,0},{64,80},{80,96},{96,112},{112,64},{1... | collective-permute-start | bytes 1572872 | tf_op jit(solution)/shard_map/ppermute | solution.py:36
  108.8 39.7 %collective-permute-start.28 = (bf16[128,4096]{1,0:T(8,128)(2,1)}, bf16[128,4096]{1,0:T(8,128)(2,1)}, u32[]{:S(2)}, u32[]{:S(2)}) collective-permute-start(bf16[128,4096]{1,0:T(8,128)(2,1)} %pad_maximum_fusion), channel_id=1, source_target_pairs={{0,1},{1,0},{2,3},{3,2},{4,5},{5,4},{6,7},{7,6},{8,9},{9,8},{10,11... | collective-permute-start | bytes 3145736 | tf_op jit(solution)/shard_map/ppermute | solution.py:36
  (37 other events, 880.9 us)

commit v3 on v2

--- a/solution.py
+++ b/solution.py
@@ -82,14 +82,14 @@
     )
 
 
-def multiply(a_parts, a_rows, j_groups, out):
+def multiply(numbers, a_parts, a_rows, j_groups, out):
     depth = a_parts[0].shape[1]
     pieces = [(p, t) for p, part in enumerate(a_parts) for t in range(part.shape[0] // PIECE)]
     tiles = [pieces[i : i + 8] for i in range(0, len(pieces), 8)]
     sizes = [len(g[1]) for g in j_groups]
     n_a, n_j, n_g = len(a_parts), sum(sizes), len(j_groups)
     width = 4 * LANES
-    numbers = jnp.stack(list(a_rows) + [x for g in j_groups for x in g[2]] + [g[0] for g in j_groups]).astype(jnp.int32)
+    j_places = [x for g in j_groups for x in g[2]]
     has = out is not None
 
     def kernel(number, *refs):
@@ -100,7 +100,7 @@
             first = sum(sizes[:g])
             loads = []
             for j in range(first, first + sizes[g]):
-                to = pl.multiple_of(number[len(pieces) + j], PIECE)
+                to = pl.multiple_of(number[j_places[j]], PIECE)
                 n = j_refs[j].shape[0]
                 loads.append(pltpu.make_async_copy(j_refs[j], j_all.at[g, pl.ds(to, n)], j_sem.at[j]))
             j_loads.append(loads)
@@ -113,34 +113,38 @@
                 for i, (p, s) in enumerate(tiles[t])
             ]
 
-        for c in j_loads[0] + a_load(0) + sum(j_loads[1:], []):
+        for c in j_loads[0] + a_load(0):
             c.start()
         pending = [[], []]
         step = 0
         for t, tile in enumerate(tiles):
             for c in a_load(t):
                 c.wait()
+            if t == 0:
+                for c in j_loads[0]:
+                    c.wait()
+                for c in sum(j_loads[1:], []):
+                    c.start()
             if t + 1 < len(tiles):
                 for c in a_load(t + 1):
                     c.start()
             m = len(tile) * PIECE
             for g in range(n_g):
-                if t == 0:
+                if t == 0 and g > 0:
                     for c in j_loads[g]:
                         c.wait()
                 slot = step % 2
                 step += 1
                 for c in pending[slot]:
                     c.wait()
-                for w in range(2):
-                    product = lax.dot_general(
-                        a_buf[t % 2, :m], j_all[g, w * 256 : (w + 1) * 256, :], NT, preferred_element_type=jnp.float32
-                    )
-                    acc[slot, :m, 2 * w : 2 * w + 2, :] = product.reshape(m, 2, LANES)
-                half = number[len(pieces) + n_j + g]
+                for w in range(m // 256):
+                    at = slice(w * 256, (w + 1) * 256)
+                    product = lax.dot_general(a_buf[t % 2, at], j_all[g], NT, preferred_element_type=jnp.float32)
+                    acc[slot, at] = product.reshape(256, 4, LANES)
+                half = number[j_groups[g][0]]
                 pending[slot] = []
                 for i in range(len(tile)):
-                    to = pl.multiple_of(number[t * 8 + i], PIECE)
+                    to = pl.multiple_of(number[a_rows[t * 8 + i]], PIECE)
                     c = pltpu.make_async_copy(
                         acc.at[slot, pl.ds(i * PIECE, PIECE)], o.at[pl.ds(to, PIECE), half], o_sem.at[slot, i]
                     )
@@ -176,6 +180,27 @@
     raw = [three_index[:PIECE], three_index[PIECE:]]
     scaled = scale(three_index, occ_index, vir_index, occ_energy, vir_energy, frequency)
     two = range(2)
+    flat = lambda blocks, steps: [blocks[h][i] for i in steps for h in two]
+
+    row, col = lax.axis_index("row"), lax.axis_index("col")
+    x_hi, z, x_lo, y, core = row // 4, row % 4, col // 8, col // 2 % 4, col % 2
+    way = 1 - 2 * core
+    numbers, at = [], {}
+    for x in two:
+        for other in two:
+            k, w = (1 - core, -way) if other else (core, way)
+            for i in range(4):
+                for h in two:
+                    at["row", x, other, i, h] = len(numbers)
+                    numbers.append((((x_lo ^ x) * 4 + (y - i * w) % 4) * 2 + k) * LANES + h * PIECE)
+    for i in range(4):
+        for h in two:
+            at["place", i, h] = len(numbers)
+            numbers.append((z - i * way) % 4 * LANES + h * PIECE)
+    at["half", 0], at["half", 1] = len(numbers), len(numbers) + 1
+    numbers = jnp.stack(numbers + [x_hi, 1 - x_hi]).astype(jnp.int32)
+    rows = lambda x, other, steps: [at["row", x, other, i, h] for i in steps for h in two]
+    columns = lambda x, blocks: (at["half", x], flat(blocks, range(4)), [at["place", i, h] for i in range(4) for h in two])
 
     a_far, j_far = [send("x_lo", scaled[0])], [send("x_hi", raw[0])]
     a_far.append(send("x_lo", scaled[1], a_far[0]))
@@ -187,6 +212,8 @@
             a[h].append(send("y", a[h][-1]))
             j[h].append(send("z", j[h][-1]))
     near_done = [a[h][3] for h in two] + [j[h][3] for h in two]
+    near = flat(a, range(4))
+    near_other = send("core", jnp.concatenate(near, 0), *near_done)
     an, jn = [], []
     for h in two:
         x, v, *_ = lax.optimization_barrier((a_far[h], j_far[h], a[h][3], j[h][3]))
@@ -196,31 +223,17 @@
         for h in two:
             an[h].append(send("y", an[h][-1]))
             jn[h].append(send("z", jn[h][-1]))
-
-    flat = lambda blocks, steps: [blocks[h][i] for i in steps for h in two]
-    a_near, an_most, an_last = flat(a, range(4)), flat(an, range(3)), flat(an, [3])
-    near_other = send("core", jnp.concatenate(a_near, 0), *near_done)
-    most_other = send("core", jnp.concatenate(an_most, 0), jn[0][2], jn[1][2])
-    last_other = send("core", jnp.concatenate(an_last, 0), jn[0][3], jn[1][3])
-
-    row, col = lax.axis_index("row"), lax.axis_index("col")
-    x_hi, z, x_lo, y, core = row // 4, row % 4, col // 8, col // 2 % 4, col % 2
-    way = 1 - 2 * core
-
-    def rows(x, other, steps):
-        k, w = (1 - core, -way) if other else (core, way)
-        return [((x * 4 + (y - i * w) % 4) * 2 + k) * LANES + h * PIECE for i in steps for h in two]
-
-    places = [(z - i * way) % 4 * LANES + h * PIECE for i in range(4) for h in two]
-    j_near = (x_hi, flat(j, range(4)), places)
-    j_rest = (1 - x_hi, flat(jn, range(4)), places)
-    near = (a_near + [near_other], rows(x_lo, 0, range(4)) + rows(x_lo, 1, range(4)))
-    most = (an_most + [most_other], rows(1 - x_lo, 0, range(3)) + rows(1 - x_lo, 1, range(3)))
-    last = (an_last + [last_other], rows(1 - x_lo, 0, [3]) + rows(1 - x_lo, 1, [3]))
-    out = multiply(*near, [j_near], None)
-    out = multiply(*most, [j_near], out)
-    out = multiply(near[0] + most[0], near[1] + most[1], [j_rest], out)
-    out = multiply(*last, [j_near, j_rest], out)
+    rest = flat(an, range(4))
+    rest_other = send("core", jnp.concatenate(rest, 0), jn[0][3], jn[1][3])
+    both = [columns(0, j), columns(1, jn)]
+    out = multiply(
+        numbers,
+        near + [near_other] + rest,
+        rows(0, 0, range(4)) + rows(0, 1, range(4)) + rows(1, 0, range(4)),
+        both,
+        None,
+    )
+    out = multiply(numbers, [rest_other], rows(1, 1, range(4)), both, out)
     return out.reshape(N_COL * LANES, N_ROW, 1, LANES)
 
 

time: 157 us -> 137 us (0.87)
  waiting for transfers between devices: 39.7 us -> 22.2 us
  starting transfers between devices: 48.4 us -> 63.4 us
  Pallas kernels: 43.6 us -> 31 us
  local copies, waits for them, and re-layouts: 21.6 us -> 18.5 us
  other arithmetic: 2.27 us -> 0 us
    ppermute x31 -> x30, waiting for transfers between devices: 39.7 us -> 22.2 us  [send(): return lax.ppermute(after(block, *earlier), axis, pairs)]
    ppermute x31 -> x30, starting transfers between devices: 48.4 us -> 63.4 us  [send(): return lax.ppermute(after(block, *earlier), axis, pairs)]
    pallas_call x4 -> x2, Pallas kernels: 42.8 us -> 30.2 us  [multiply(): pl.pallas_call(kernel, out_shape=jax.ShapeDtypeStruct((N_COL * LANES, 2,...]
    concatenate x1 -> x0, other arithmetic: 2.27 us -> none  [shards(): last_other = send('core', jnp.concatenate(an_last, 0), jn[0][3], jn[1][3])]
    another operation x4 -> x1, local copies, waits for them, and re-layouts: 2.6 us -> 0.64 us  [shards(): numbers = jnp.stack(numbers + [x_hi, 1 - x_hi]).astype(jnp.int32)]
    unnamed x72 -> x84, local copies, waits for them, and re-layouts: 15.7 us -> 14.6 us
  transfers between devices with their start and end apart: 31 -> 30, of which waited for: 14 -> 8; matrix products, arithmetic and copies ran while one was open for 11% -> 11% of each run, Pallas kernels for 22% -> 14%
where the time goes in v3:
time: 137 us
  starting transfers between devices  63.4 us (46%)
  Pallas kernels  31 us (23%)
  waiting for transfers between devices  22.2 us (16%)
  local copies, waits for them, and re-layouts  18.5 us (14%)
  between operations  1.41 us (1%)
    ppermute x30, starting transfers between devices, send(): return lax.ppermute(after(block, *earlier), axis, pairs)  63.4 us
    pallas_call x2, Pallas kernels, multiply(): pl.pallas_call(kernel, out_shape=jax.ShapeDtypeStruct((N_COL * LANES, 2,...  30.2 us
    ppermute x30, waiting for transfers between devices, send(): return lax.ppermute(after(block, *earlier), axis, pairs)  22.2 us
    unnamed x84, local copies, waits for them, and re-layouts  14.6 us
  transfers between devices with their start and end apart: 30, of which 8 were waited for; matrix products, arithmetic and copies ran while one was open for 11% of the time, Pallas kernels for 14%

profile of v3, /device:TPU:1, one launch (start us, length us, event | category | flops | bytes accessed | tf_op | source)
XLA Modules:
  0.0 136.5 jit_solution(10681374222503903556)
XLA Ops:
  5.6 3.6 %collective-permute-start.2 = (bf16[64,4096]{1,0:T(8,128)(2,1)S(1)}, bf16[64,4096]{1,0:T(8,128)(2,1)S(1)}, u32[]{:S(2)}, u32[]{:S(2)}) collective-permute-start(bf16[64,4096]{1,0:T(8,128)(2,1)S(1)} %get-tuple-element.15.refs_0_), channel_id=1, source_target_pairs={{0,2},{1,7},{2,4},{3,1},{4,6},{5,3},{6,0},{7,5},{8,10},{9,15},{10,... | collective-permute-start | bytes 1572872 | tf_op jit(solution)/shard_map/ppermute | solution.py:36
  11.0 3.8 %collective-permute-start.13 = (bf16[64,4096]{1,0:T(8,128)(2,1)S(1)}, bf16[64,4096]{1,0:T(8,128)(2,1)S(1)}, u32[]{:S(2)}, u32[]{:S(2)}) collective-permute-start(bf16[64,4096]{1,0:T(8,128)(2,1)S(1)} %get-tuple-element.19.refs_18_.refs_2_), channel_id=1, source_target_pairs={{0,16},{16,32},{32,48},{48,0},{64,80},{80,96},{96,112},{112,64},{1... | collective-permute-start | bytes 1572872 | tf_op jit(solution)/shard_map/ppermute | solution.py:36
  15.8 3.0 %collective-permute-start.3 = (bf16[64,4096]{1,0:T(8,128)(2,1)S(1)}, bf16[64,4096]{1,0:T(8,128)(2,1)S(1)}, u32[]{:S(2)}, u32[]{:S(2)}) collective-permute-start(bf16[64,4096]{1,0:T(8,128)(2,1)S(1)} %collective-permute-done.2.refs_2_), channel_id=1, source_target_pairs={{0,2},{1,7},{2,4},{3,1},{4,6},{5,3},{6,0},{7,5},{8,10},{9,15},{10,... | collective-permute-start | bytes 1572872 | tf_op jit(solution)/shard_map/ppermute | solution.py:36
  19.6 1.4 %collective-permute-done.10.refs_3_ = bf16[64,4096]{1,0:T(8,128)(2,1)S(1)} collective-permute-done((bf16[64,4096]{1,0:T(8,128)(2,1)S(1)}, bf16[64,4096]{1,0:T(8,128)(2,1)S(1)}, u32[]{:S(2)}, u32[]{:S(2)}) %collective-permute-start.10) | collective-permute-done | bytes 524320 | tf_op jit(solution)/shard_map/ppermute | solution.py:36
  21.0 2.7 %collective-permute-start.1 = (bf16[64,4096]{1,0:T(8,128)(2,1)S(1)}, bf16[64,4096]{1,0:T(8,128)(2,1)S(1)}, u32[]{:S(2)}, u32[]{:S(2)}) collective-permute-start(bf16[64,4096]{1,0:T(8,128)(2,1)S(1)} %get-tuple-element.26.refs_17_.refs_1_), channel_id=1, source_target_pairs={{0,64},{16,80},{32,96},{48,112},{64,0},{80,16},{96,32},{112,48},{1... | collective-permute-start | bytes 1572872 | tf_op jit(solution)/shard_map/ppermute | solution.py:36
  23.7 2.9 %collective-permute-done.5.refs_19_.refs_3_ = bf16[64,4096]{1,0:T(8,128)(2,1)S(1)} collective-permute-done((bf16[64,4096]{1,0:T(8,128)(2,1)S(1)}, bf16[64,4096]{1,0:T(8,128)(2,1)S(1)}, u32[]{:S(2)}, u32[]{:S(2)}) %collective-permute-start.5) | collective-permute-done | bytes 524320 | tf_op jit(solution)/shard_map/ppermute | solution.py:36
  26.6 3.4 %collective-permute-start.6 = (bf16[64,4096]{1,0:T(8,128)(2,1)S(1)}, bf16[64,4096]{1,0:T(8,128)(2,1)S(1)}, u32[]{:S(2)}, u32[]{:S(2)}) collective-permute-start(bf16[64,4096]{1,0:T(8,128)(2,1)S(1)} %collective-permute-done.5.refs_19_.refs_3_), channel_id=1, source_target_pairs={{0,16},{16,32},{32,48},{48,0},{64,80},{80,96},{96,112},{112,64},{1... | collective-permute-start | bytes 1572872 | tf_op jit(solution)/shard_map/ppermute | solution.py:36
  32.6 1.5 %collective-permute-done.1.refs_25_.refs_9_ = bf16[64,4096]{1,0:T(8,128)(2,1)S(1)} collective-permute-done((bf16[64,4096]{1,0:T(8,128)(2,1)S(1)}, bf16[64,4096]{1,0:T(8,128)(2,1)S(1)}, u32[]{:S(2)}, u32[]{:S(2)}) %collective-permute-start.1) | collective-permute-done | bytes 524320 | tf_op jit(solution)/shard_map/ppermute | solution.py:36
  36.1 3.4 %collective-permute-start.7 = (bf16[64,4096]{1,0:T(8,128)(2,1)S(1)}, bf16[64,4096]{1,0:T(8,128)(2,1)S(1)}, u32[]{:S(2)}, u32[]{:S(2)}) collective-permute-start(bf16[64,4096]{1,0:T(8,128)(2,1)S(1)} %collective-permute-done.6.refs_21_.refs_5_), channel_id=1, source_target_pairs={{0,16},{16,32},{32,48},{48,0},{64,80},{80,96},{96,112},{112,64},{1... | collective-permute-start | bytes 1572872 | tf_op jit(solution)/shard_map/ppermute | solution.py:36
  40.3 2.5 %collective-permute-start.9 = (bf16[64,4096]{1,0:T(8,128)(2,1)S(1)}, bf16[64,4096]{1,0:T(8,128)(2,1)S(1)}, u32[]{:S(2)}, u32[]{:S(2)}) collective-permute-start(bf16[64,4096]{1,0:T(8,128)(2,1)S(1)} %get-tuple-element.19.refs_18_.refs_2_), channel_id=1, source_target_pairs={{0,64},{16,80},{32,96},{48,112},{64,0},{80,16},{96,32},{112,48},{1... | collective-permute-start | bytes 1572872 | tf_op jit(solution)/shard_map/ppermute | solution.py:36
  42.8 3.9 %collective-permute-start.12 = (bf16[64,4096]{1,0:T(8,128)(2,1)S(1)}, bf16[64,4096]{1,0:T(8,128)(2,1)S(1)}, u32[]{:S(2)}, u32[]{:S(2)}) collective-permute-start(bf16[64,4096]{1,0:T(8,128)(2,1)S(1)} %collective-permute-done.11.refs_5_), channel_id=1, source_target_pairs={{0,2},{1,7},{2,4},{3,1},{4,6},{5,3},{6,0},{7,5},{8,10},{9,15},{10,... | collective-permute-start | bytes 1572872 | tf_op jit(solution)/shard_map/ppermute | solution.py:36
  47.8 1.8 %collective-permute-start.16 = (bf16[64,4096]{1,0:T(8,128)(2,1)S(1)}, bf16[64,4096]{1,0:T(8,128)(2,1)S(1)}, u32[]{:S(2)}, u32[]{:S(2)}) collective-permute-start(bf16[64,4096]{1,0:T(8,128)(2,1)S(1)} %collective-permute-done.refs_9_), channel_id=1, source_target_pairs={{0,2},{1,7},{2,4},{3,1},{4,6},{5,3},{6,0},{7,5},{8,10},{9,15},{10,... | collective-permute-start | bytes 1572872 | tf_op jit(solution)/shard_map/ppermute | solution.py:36
  50.4 7.0 %collective-permute-done.9.refs_26_.refs_10_ = bf16[64,4096]{1,0:T(8,128)(2,1)S(1)} collective-permute-done((bf16[64,4096]{1,0:T(8,128)(2,1)S(1)}, bf16[64,4096]{1,0:T(8,128)(2,1)S(1)}, u32[]{:S(2)}, u32[]{:S(2)}) %collective-permute-start.9) | collective-permute-done | bytes 524320 | tf_op jit(solution)/shard_map/ppermute | solution.py:36
  57.4 3.8 %collective-permute-start.25 = (bf16[64,4096]{1,0:T(8,128)(2,1)S(1)}, bf16[64,4096]{1,0:T(8,128)(2,1)S(1)}, u32[]{:S(2)}, u32[]{:S(2)}) collective-permute-start(bf16[64,4096]{1,0:T(8,128)(2,1)S(1)} %collective-permute-done.9.refs_26_.refs_10_), channel_id=1, source_target_pairs={{0,16},{16,32},{32,48},{48,0},{64,80},{80,96},{96,112},{112,64},{1... | collective-permute-start | bytes 1572872 | tf_op jit(solution)/shard_map/ppermute | solution.py:36
  61.2 6.4 %collective-permute-start.17 = (bf16[64,4096]{1,0:T(8,128)(2,1)S(1)}, bf16[64,4096]{1,0:T(8,128)(2,1)S(1)}, u32[]{:S(2)}, u32[]{:S(2)}) collective-permute-start(bf16[64,4096]{1,0:T(8,128)(2,1)S(1)} %collective-permute-done.8.refs_10_), channel_id=1, source_target_pairs={{0,2},{1,7},{2,4},{3,1},{4,6},{5,3},{6,0},{7,5},{8,10},{9,15},{10,... | collective-permute-start | bytes 1572872 | tf_op jit(solution)/shard_map/ppermute | solution.py:36
  70.7 3.1 %collective-permute-done.17.refs_12_ = bf16[64,4096]{1,0:T(8,128)(2,1)S(1)} collective-permute-done((bf16[64,4096]{1,0:T(8,128)(2,1)S(1)}, bf16[64,4096]{1,0:T(8,128)(2,1)S(1)}, u32[]{:S(2)}, u32[]{:S(2)}) %collective-permute-start.17) | collective-permute-done | bytes 524320 | tf_op jit(solution)/shard_map/ppermute | solution.py:36
  73.8 3.4 %collective-permute-start.19 = (bf16[64,4096]{1,0:T(8,128)(2,1)S(1)}, bf16[64,4096]{1,0:T(8,128)(2,1)S(1)}, u32[]{:S(2)}, u32[]{:S(2)}) collective-permute-start(bf16[64,4096]{1,0:T(8,128)(2,1)S(1)} %collective-permute-done.17.refs_12_), channel_id=1, source_target_pairs={{0,2},{1,7},{2,4},{3,1},{4,6},{5,3},{6,0},{7,5},{8,10},{9,15},{10,... | collective-permute-start | bytes 1572872 | tf_op jit(solution)/shard_map/ppermute | solution.py:36
  77.2 5.3 %collective-permute-start.18 = (bf16[64,4096]{1,0:T(8,128)(2,1)S(1)}, bf16[64,4096]{1,0:T(8,128)(2,1)S(1)}, u32[]{:S(2)}, u32[]{:S(2)}) collective-permute-start(bf16[64,4096]{1,0:T(8,128)(2,1)S(1)} %collective-permute-done.16.refs_11_), channel_id=1, source_target_pairs={{0,2},{1,7},{2,4},{3,1},{4,6},{5,3},{6,0},{7,5},{8,10},{9,15},{10,... | collective-permute-start | bytes 1572872 | tf_op jit(solution)/shard_map/ppermute | solution.py:36
  84.4 3.7 %collective-permute-start.21 = (bf16[64,4096]{1,0:T(8,128)(2,1)S(1)}, bf16[64,4096]{1,0:T(8,128)(2,1)S(1)}, u32[]{:S(2)}, u32[]{:S(2)}) collective-permute-start(bf16[64,4096]{1,0:T(8,128)(2,1)S(1)} %collective-permute-done.19.refs_14_), channel_id=1, source_target_pairs={{0,2},{1,7},{2,4},{3,1},{4,6},{5,3},{6,0},{7,5},{8,10},{9,15},{10,... | collective-permute-start | bytes 1572872 | tf_op jit(solution)/shard_map/ppermute | solution.py:36
  88.9 4.8 %collective-permute-start.20 = (bf16[64,4096]{1,0:T(8,128)(2,1)S(1)}, bf16[64,4096]{1,0:T(8,128)(2,1)S(1)}, u32[]{:S(2)}, u32[]{:S(2)}) collective-permute-start(bf16[64,4096]{1,0:T(8,128)(2,1)S(1)} %collective-permute-done.18.refs_13_), channel_id=1, source_target_pairs={{0,2},{1,7},{2,4},{3,1},{4,6},{5,3},{6,0},{7,5},{8,10},{9,15},{10,... | collective-permute-start | bytes 1572872 | tf_op jit(solution)/shard_map/ppermute | solution.py:36
  95.4 4.7 %collective-permute-done.20.refs_15_ = bf16[64,4096]{1,0:T(8,128)(2,1)S(1)} collective-permute-done((bf16[64,4096]{1,0:T(8,128)(2,1)S(1)}, bf16[64,4096]{1,0:T(8,128)(2,1)S(1)}, u32[]{:S(2)}, u32[]{:S(2)}) %collective-permute-start.20) | collective-permute-done | bytes 524320 | tf_op jit(solution)/shard_map/ppermute | solution.py:36
  102.2 3.0 %collective-permute-start.28 = (bf16[512,4096]{1,0:T(8,128)(2,1)}, bf16[512,4096]{1,0:T(8,128)(2,1)}, u32[]{:S(2)}, u32[]{:S(2)}) collective-permute-start(bf16[512,4096]{1,0:T(8,128)(2,1)} %constant_dynamic-update-slice_fusion), channel_id=1, source_target_pairs={{0,1},{1,0},{2,3},{3,2},{4,5},{5,4},{6,7},{7,6},{8,9},{9,8},{10,11... | collective-permute-start | bytes 12582920 | tf_op jit(solution)/shard_map/ppermute | solution.py:36
  106.2 19.7 %shard_map.65.refs_17_ = f32[2048,2,4,128]{3,2,1,0:T(4,128)} custom-call(s32[42]{0:T(128)} %stack.171.number, bf16[64,4096]{1,0:T(8,128)(2,1)} %copy-done.1, bf16[64,4096]{1,0:T(8,128)(2,1)} %copy-done.2, bf16[64,4096]{1,0:T(8,128)(2,1)} %copy-done.21, bf16[64,4096]{1,0:T(8,128)(2,1)} %copy-done.23, bf16[64,4096]{1,0:T(8,128)(2,1)} %copy-done.24, ...), custom_call_target="tpu_custom_call" | custom-call | flops 12884901888 | bytes 16777216 | tf_op jit(solution)/shard_map/pallas_call | solution.py:158
  125.9 10.4 %shard_map.66 = f32[2048,2,4,128]{3,2,1,0:T(4,128)} custom-call(s32[42]{0:T(128)} %stack.171.number, bf16[512,4096]{1,0:T(8,128)(2,1)} %collective-permute-done.28.refs_0_, bf16[64,4096]{1,0:T(8,128)(2,1)} %copy-done.6, bf16[64,4096]{1,0:T(8,128)(2,1)} %copy-done.5, bf16[64,4096]{1,0:T(8,128)(2,1)} %copy-done.8, ...), custom_call_target="tpu_custom_call", output_to_operand_aliasing={{}: (18, {})} | custom-call | flops 4294967296 | bytes 16777216 | tf_op jit(solution)/shard_map/pallas_call | solution.py:158
  (129 shorter events, 25.7 us)
Async XLA Ops:
  9.2 22.2 %collective-permute-start = (bf16[64,4096]{1,0:T(8,128)(2,1)S(1)}, bf16[64,4096]{1,0:T(8,128)(2,1)S(1)}, u32[]{:S(2)}, u32[]{:S(2)}) collective-permute-start(bf16[64,4096]{1,0:T(8,128)(2,1)S(1)} %get-tuple-element.15.refs_0_), channel_id=1, source_target_pairs={{0,8},{1,9},{2,10},{3,11},{4,12},{5,13},{6,14},{7,15},{8,0},{9,1},... | collective-permute-start | bytes 1572872 | tf_op jit(solution)/shard_map/ppermute | solution.py:36
  11.0 19.8 %collective-permute-start.13 = (bf16[64,4096]{1,0:T(8,128)(2,1)S(1)}, bf16[64,4096]{1,0:T(8,128)(2,1)S(1)}, u32[]{:S(2)}, u32[]{:S(2)}) collective-permute-start(bf16[64,4096]{1,0:T(8,128)(2,1)S(1)} %get-tuple-element.19.refs_18_.refs_2_), channel_id=1, source_target_pairs={{0,16},{16,32},{32,48},{48,0},{64,80},{80,96},{96,112},{112,64},{1... | collective-permute-start | bytes 1572872 | tf_op jit(solution)/shard_map/ppermute | solution.py:36
  14.8 11.7 %collective-permute-start.5 = (bf16[64,4096]{1,0:T(8,128)(2,1)S(1)}, bf16[64,4096]{1,0:T(8,128)(2,1)S(1)}, u32[]{:S(2)}, u32[]{:S(2)}) collective-permute-start(bf16[64,4096]{1,0:T(8,128)(2,1)S(1)} %get-tuple-element.26.refs_17_.refs_1_), channel_id=1, source_target_pairs={{0,16},{16,32},{32,48},{48,0},{64,80},{80,96},{96,112},{112,64},{1... | collective-permute-start | bytes 1572872 | tf_op jit(solution)/shard_map/ppermute | solution.py:36
  15.8 15.8 %collective-permute-start.3 = (bf16[64,4096]{1,0:T(8,128)(2,1)S(1)}, bf16[64,4096]{1,0:T(8,128)(2,1)S(1)}, u32[]{:S(2)}, u32[]{:S(2)}) collective-permute-start(bf16[64,4096]{1,0:T(8,128)(2,1)S(1)} %collective-permute-done.2.refs_2_), channel_id=1, source_target_pairs={{0,2},{1,7},{2,4},{3,1},{4,6},{5,3},{6,0},{7,5},{8,10},{9,15},{10,... | collective-permute-start | bytes 1572872 | tf_op jit(solution)/shard_map/ppermute | solution.py:36
  21.0 13.1 %collective-permute-start.1 = (bf16[64,4096]{1,0:T(8,128)(2,1)S(1)}, bf16[64,4096]{1,0:T(8,128)(2,1)S(1)}, u32[]{:S(2)}, u32[]{:S(2)}) collective-permute-start(bf16[64,4096]{1,0:T(8,128)(2,1)S(1)} %get-tuple-element.26.refs_17_.refs_1_), channel_id=1, source_target_pairs={{0,64},{16,80},{32,96},{48,112},{64,0},{80,16},{96,32},{112,48},{1... | collective-permute-start | bytes 1572872 | tf_op jit(solution)/shard_map/ppermute | solution.py:36
  31.4 11.4 %collective-permute-start.14 = (bf16[64,4096]{1,0:T(8,128)(2,1)S(1)}, bf16[64,4096]{1,0:T(8,128)(2,1)S(1)}, u32[]{:S(2)}, u32[]{:S(2)}) collective-permute-start(bf16[64,4096]{1,0:T(8,128)(2,1)S(1)} %collective-permute-done.13.refs_20_.refs_4_), channel_id=1, source_target_pairs={{0,16},{16,32},{32,48},{48,0},{64,80},{80,96},{96,112},{112,64},{1... | collective-permute-start | bytes 1572872 | tf_op jit(solution)/shard_map/ppermute | solution.py:36
  31.6 15.2 %collective-permute-start.4 = (bf16[64,4096]{1,0:T(8,128)(2,1)S(1)}, bf16[64,4096]{1,0:T(8,128)(2,1)S(1)}, u32[]{:S(2)}, u32[]{:S(2)}) collective-permute-start(bf16[64,4096]{1,0:T(8,128)(2,1)S(1)} %collective-permute-done.3.refs_4_), channel_id=1, source_target_pairs={{0,2},{1,7},{2,4},{3,1},{4,6},{5,3},{6,0},{7,5},{8,10},{9,15},{10,... | collective-permute-start | bytes 1572872 | tf_op jit(solution)/shard_map/ppermute | solution.py:36
  34.1 16.3 %collective-permute-start.8 = (bf16[64,4096]{1,0:T(8,128)(2,1)S(1)}, bf16[64,4096]{1,0:T(8,128)(2,1)S(1)}, u32[]{:S(2)}, u32[]{:S(2)}) collective-permute-start(bf16[64,4096]{1,0:T(8,128)(2,1)S(1)} %get-tuple-element.18.refs_1_), channel_id=1, source_target_pairs={{0,8},{1,9},{2,10},{3,11},{4,12},{5,13},{6,14},{7,15},{8,0},{9,1},... | collective-permute-start | bytes 1572872 | tf_op jit(solution)/shard_map/ppermute | solution.py:36
  36.1 11.7 %collective-permute-start.7 = (bf16[64,4096]{1,0:T(8,128)(2,1)S(1)}, bf16[64,4096]{1,0:T(8,128)(2,1)S(1)}, u32[]{:S(2)}, u32[]{:S(2)}) collective-permute-start(bf16[64,4096]{1,0:T(8,128)(2,1)S(1)} %collective-permute-done.6.refs_21_.refs_5_), channel_id=1, source_target_pairs={{0,16},{16,32},{32,48},{48,0},{64,80},{80,96},{96,112},{112,64},{1... | collective-permute-start | bytes 1572872 | tf_op jit(solution)/shard_map/ppermute | solution.py:36
  40.3 17.0 %collective-permute-start.9 = (bf16[64,4096]{1,0:T(8,128)(2,1)S(1)}, bf16[64,4096]{1,0:T(8,128)(2,1)S(1)}, u32[]{:S(2)}, u32[]{:S(2)}) collective-permute-start(bf16[64,4096]{1,0:T(8,128)(2,1)S(1)} %get-tuple-element.19.refs_18_.refs_2_), channel_id=1, source_target_pairs={{0,64},{16,80},{32,96},{48,112},{64,0},{80,16},{96,32},{112,48},{1... | collective-permute-start | bytes 1572872 | tf_op jit(solution)/shard_map/ppermute | solution.py:36
  42.8 14.6 %collective-permute-start.12 = (bf16[64,4096]{1,0:T(8,128)(2,1)S(1)}, bf16[64,4096]{1,0:T(8,128)(2,1)S(1)}, u32[]{:S(2)}, u32[]{:S(2)}) collective-permute-start(bf16[64,4096]{1,0:T(8,128)(2,1)S(1)} %collective-permute-done.11.refs_5_), channel_id=1, source_target_pairs={{0,2},{1,7},{2,4},{3,1},{4,6},{5,3},{6,0},{7,5},{8,10},{9,15},{10,... | collective-permute-start | bytes 1572872 | tf_op jit(solution)/shard_map/ppermute | solution.py:36
  46.7 10.7 %collective-permute-start.15 = (bf16[64,4096]{1,0:T(8,128)(2,1)S(1)}, bf16[64,4096]{1,0:T(8,128)(2,1)S(1)}, u32[]{:S(2)}, u32[]{:S(2)}) collective-permute-start(bf16[64,4096]{1,0:T(8,128)(2,1)S(1)} %collective-permute-done.14.refs_22_.refs_6_), channel_id=1, source_target_pairs={{0,16},{16,32},{32,48},{48,0},{64,80},{80,96},{96,112},{112,64},{1... | collective-permute-start | bytes 1572872 | tf_op jit(solution)/shard_map/ppermute | solution.py:36
  47.8 29.5 %collective-permute-start.16 = (bf16[64,4096]{1,0:T(8,128)(2,1)S(1)}, bf16[64,4096]{1,0:T(8,128)(2,1)S(1)}, u32[]{:S(2)}, u32[]{:S(2)}) collective-permute-start(bf16[64,4096]{1,0:T(8,128)(2,1)S(1)} %collective-permute-done.refs_9_), channel_id=1, source_target_pairs={{0,2},{1,7},{2,4},{3,1},{4,6},{5,3},{6,0},{7,5},{8,10},{9,15},{10,... | collective-permute-start | bytes 1572872 | tf_op jit(solution)/shard_map/ppermute | solution.py:36
  57.4 12.9 %collective-permute-start.25 = (bf16[64,4096]{1,0:T(8,128)(2,1)S(1)}, bf16[64,4096]{1,0:T(8,128)(2,1)S(1)}, u32[]{:S(2)}, u32[]{:S(2)}) collective-permute-start(bf16[64,4096]{1,0:T(8,128)(2,1)S(1)} %collective-permute-done.9.refs_26_.refs_10_), channel_id=1, source_target_pairs={{0,16},{16,32},{32,48},{48,0},{64,80},{80,96},{96,112},{112,64},{1... | collective-permute-start | bytes 1572872 | tf_op jit(solution)/shard_map/ppermute | solution.py:36
  61.2 12.6 %collective-permute-start.17 = (bf16[64,4096]{1,0:T(8,128)(2,1)S(1)}, bf16[64,4096]{1,0:T(8,128)(2,1)S(1)}, u32[]{:S(2)}, u32[]{:S(2)}) collective-permute-start(bf16[64,4096]{1,0:T(8,128)(2,1)S(1)} %collective-permute-done.8.refs_10_), channel_id=1, source_target_pairs={{0,2},{1,7},{2,4},{3,1},{4,6},{5,3},{6,0},{7,5},{8,10},{9,15},{10,... | collective-permute-start | bytes 1572872 | tf_op jit(solution)/shard_map/ppermute | solution.py:36
  69.5 36.7 %collective-permute-start.29 = (bf16[512,4096]{1,0:T(8,128)(2,1)}, bf16[512,4096]{1,0:T(8,128)(2,1)}, u32[]{:S(2)}, u32[]{:S(2)}) collective-permute-start(bf16[512,4096]{1,0:T(8,128)(2,1)} %constant_dynamic-update-slice_fusion.8), channel_id=1, source_target_pairs={{0,1},{1,0},{2,3},{3,2},{4,5},{5,4},{6,7},{7,6},{8,9},{9,8},{10,11... | collective-permute-start | bytes 12582920 | tf_op jit(solution)/shard_map/ppermute | solution.py:36
  70.3 13.9 %collective-permute-start.26 = (bf16[64,4096]{1,0:T(8,128)(2,1)S(1)}, bf16[64,4096]{1,0:T(8,128)(2,1)S(1)}, u32[]{:S(2)}, u32[]{:S(2)}) collective-permute-start(bf16[64,4096]{1,0:T(8,128)(2,1)S(1)} %collective-permute-done.25.refs_28_.refs_12_), channel_id=1, source_target_pairs={{0,16},{16,32},{32,48},{48,0},{64,80},{80,96},{96,112},{112,64},{1... | collective-permute-start | bytes 1572872 | tf_op jit(solution)/shard_map/ppermute | solution.py:36
  77.2 10.9 %collective-permute-start.23 = (bf16[64,4096]{1,0:T(8,128)(2,1)S(1)}, bf16[64,4096]{1,0:T(8,128)(2,1)S(1)}, u32[]{:S(2)}, u32[]{:S(2)}) collective-permute-start(bf16[64,4096]{1,0:T(8,128)(2,1)S(1)} %collective-permute-done.22.refs_27_.refs_11_), channel_id=1, source_target_pairs={{0,16},{16,32},{32,48},{48,0},{64,80},{80,96},{96,112},{112,64},{1... | collective-permute-start | bytes 1572872 | tf_op jit(solution)/shard_map/ppermute | solution.py:36
  77.2 11.7 %collective-permute-start.18 = (bf16[64,4096]{1,0:T(8,128)(2,1)S(1)}, bf16[64,4096]{1,0:T(8,128)(2,1)S(1)}, u32[]{:S(2)}, u32[]{:S(2)}) collective-permute-start(bf16[64,4096]{1,0:T(8,128)(2,1)S(1)} %collective-permute-done.16.refs_11_), channel_id=1, source_target_pairs={{0,2},{1,7},{2,4},{3,1},{4,6},{5,3},{6,0},{7,5},{8,10},{9,15},{10,... | collective-permute-start | bytes 1572872 | tf_op jit(solution)/shard_map/ppermute | solution.py:36
  84.3 17.9 %collective-permute-start.27 = (bf16[64,4096]{1,0:T(8,128)(2,1)S(1)}, bf16[64,4096]{1,0:T(8,128)(2,1)S(1)}, u32[]{:S(2)}, u32[]{:S(2)}) collective-permute-start(bf16[64,4096]{1,0:T(8,128)(2,1)S(1)} %collective-permute-done.26.refs_30_.refs_14_), channel_id=1, source_target_pairs={{0,16},{16,32},{32,48},{48,0},{64,80},{80,96},{96,112},{112,64},{1... | collective-permute-start | bytes 1572872 | tf_op jit(solution)/shard_map/ppermute | solution.py:36
  84.4 16.7 %collective-permute-start.21 = (bf16[64,4096]{1,0:T(8,128)(2,1)S(1)}, bf16[64,4096]{1,0:T(8,128)(2,1)S(1)}, u32[]{:S(2)}, u32[]{:S(2)}) collective-permute-start(bf16[64,4096]{1,0:T(8,128)(2,1)S(1)} %collective-permute-done.19.refs_14_), channel_id=1, source_target_pairs={{0,2},{1,7},{2,4},{3,1},{4,6},{5,3},{6,0},{7,5},{8,10},{9,15},{10,... | collective-permute-start | bytes 1572872 | tf_op jit(solution)/shard_map/ppermute | solution.py:36
  88.2 14.0 %collective-permute-start.24 = (bf16[64,4096]{1,0:T(8,128)(2,1)S(1)}, bf16[64,4096]{1,0:T(8,128)(2,1)S(1)}, u32[]{:S(2)}, u32[]{:S(2)}) collective-permute-start(bf16[64,4096]{1,0:T(8,128)(2,1)S(1)} %collective-permute-done.23.refs_29_.refs_13_), channel_id=1, source_target_pairs={{0,16},{16,32},{32,48},{48,0},{64,80},{80,96},{96,112},{112,64},{1... | collective-permute-start | bytes 1572872 | tf_op jit(solution)/shard_map/ppermute | solution.py:36
  88.9 11.2 %collective-permute-start.20 = (bf16[64,4096]{1,0:T(8,128)(2,1)S(1)}, bf16[64,4096]{1,0:T(8,128)(2,1)S(1)}, u32[]{:S(2)}, u32[]{:S(2)}) collective-permute-start(bf16[64,4096]{1,0:T(8,128)(2,1)S(1)} %collective-permute-done.18.refs_13_), channel_id=1, source_target_pairs={{0,2},{1,7},{2,4},{3,1},{4,6},{5,3},{6,0},{7,5},{8,10},{9,15},{10,... | collective-permute-start | bytes 1572872 | tf_op jit(solution)/shard_map/ppermute | solution.py:36
  102.2 23.8 %collective-permute-start.28 = (bf16[512,4096]{1,0:T(8,128)(2,1)}, bf16[512,4096]{1,0:T(8,128)(2,1)}, u32[]{:S(2)}, u32[]{:S(2)}) collective-permute-start(bf16[512,4096]{1,0:T(8,128)(2,1)} %constant_dynamic-update-slice_fusion), channel_id=1, source_target_pairs={{0,1},{1,0},{2,3},{3,2},{4,5},{5,4},{6,7},{7,6},{8,9},{9,8},{10,11... | collective-permute-start | bytes 12582920 | tf_op jit(solution)/shard_map/ppermute | solution.py:36
  (41 other events, 1225.5 us)

commit v4 on v3

--- a/solution.py
+++ b/solution.py
@@ -43,43 +43,54 @@
 def scale(three_index, occ_index, vir_index, occ_energy, vir_energy, frequency):
     rows, pairs = three_index.shape
     chunks = pairs // LANES
-
-    def table(energy):
-        padded = -(-energy.shape[0] // (8 * LANES)) * 8 * LANES
-        return jnp.pad(energy, (0, padded - energy.shape[0])).reshape(-1, LANES)
-
-    def kernel(freq, occ, vir, occ_table, vir_table, b, *outs):
-        def look_up(table_ref, index):
+    lines = [-(-e.shape[0] // LANES) for e in (vir_energy, occ_energy)]
+
+    def padded(energy):
+        return jnp.pad(energy, (0, -energy.shape[0] % LANES))
+
+    tables = jnp.concatenate([padded(vir_energy), padded(occ_energy)]).reshape(-1, LANES)
+
+    def kernel(freq, *refs):
+        sources, outs, buffers, sem = refs[:4], refs[4:6], refs[6:10], refs[10]
+        loads = [pltpu.make_async_copy(s, d, sem.at[i]) for i, (s, d) in enumerate(zip(sources, buffers))]
+        for c in loads:
+            c.start()
+        for c in loads[:3]:
+            c.wait()
+        occ, vir, table, b = buffers
+
+        def look_up(first, count, index):
             high, low = index >> 7, index & (LANES - 1)
             found = jnp.zeros(index.shape, jnp.float32)
-            for k in range(table_ref.shape[0]):
-                line = jnp.broadcast_to(table_ref[k : k + 1, :], index.shape)
+            for k in range(count):
+                line = jnp.broadcast_to(table[first + k : first + k + 1, :], index.shape)
                 found = jnp.where(high == k, jnp.take_along_axis(line, low, axis=1), found)
             return found
 
-        gap = look_up(vir_table, vir[...]) - look_up(occ_table, occ[...])
+        gap = look_up(0, lines[0], vir[...]) - look_up(lines[0], lines[1], occ[...])
         denominator = -4.0 * gap / (gap * gap + freq[0] * freq[0])
+        loads[3].wait()
         for k in range(chunks):
             at = slice(k * LANES, (k + 1) * LANES)
             scaled = (b[:, at].astype(jnp.float32) * denominator[k : k + 1, :]).astype(jnp.bfloat16)
             for h, out in enumerate(outs):
                 out[:, at] = scaled[h * PIECE : (h + 1) * PIECE]
 
-    vmem = pl.BlockSpec(memory_space=pltpu.VMEM)
+    vmem, hbm = pl.BlockSpec(memory_space=pltpu.VMEM), pl.BlockSpec(memory_space=pl.ANY)
     return pl.pallas_call(
         kernel,
         out_shape=[jax.ShapeDtypeStruct((PIECE, pairs), jnp.bfloat16)] * 2,
-        in_specs=[pl.BlockSpec(memory_space=pltpu.SMEM)] + [vmem] * 5,
+        in_specs=[pl.BlockSpec(memory_space=pltpu.SMEM)] + [hbm] * 4,
         out_specs=[vmem] * 2,
-        compiler_params=pltpu.CompilerParams(vmem_limit_bytes=32 << 20),
-    )(
-        frequency,
-        occ_index.reshape(chunks, LANES),
-        vir_index.reshape(chunks, LANES),
-        table(occ_energy),
-        table(vir_energy),
-        three_index,
-    )
+        scratch_shapes=[
+            pltpu.VMEM((chunks, LANES), jnp.int32),
+            pltpu.VMEM((chunks, LANES), jnp.int32),
+            pltpu.VMEM((sum(lines), LANES), jnp.float32),
+            pltpu.VMEM((rows, pairs), jnp.bfloat16),
+            pltpu.SemaphoreType.DMA((4,)),
+        ],
+        compiler_params=pltpu.CompilerParams(vmem_limit_bytes=VMEM),
+    )(frequency, occ_index.reshape(chunks, LANES), vir_index.reshape(chunks, LANES), tables, three_index)
 
 
 def multiply(numbers, a_parts, a_rows, j_groups, out):
@@ -207,13 +218,15 @@
     j_far.append(send("x_hi", raw[1], j_far[0]))
     a = [[scaled[h]] for h in two]
     j = [[raw[h]] for h in two]
-    for _ in range(3):
+    for i in range(3):
         for h in two:
-            a[h].append(send("y", a[h][-1]))
-            j[h].append(send("z", j[h][-1]))
+            crossed = [a_far[0], j_far[0]] if i == 2 else []
+            x, v, *_ = lax.optimization_barrier((a[h][-1], j[h][-1], *crossed)) if i else (a[h][-1], j[h][-1])
+            a[h].append(send("y", x))
+            j[h].append(send("z", v))
     near_done = [a[h][3] for h in two] + [j[h][3] for h in two]
     near = flat(a, range(4))
-    near_other = send("core", jnp.concatenate(near, 0), *near_done)
+    near_other = send("core", jnp.concatenate(near, 0), *near_done, numbers)
     an, jn = [], []
     for h in two:
         x, v, *_ = lax.optimization_barrier((a_far[h], j_far[h], a[h][3], j[h][3]))
@@ -221,8 +234,9 @@
         jn.append([v])
     for _ in range(3):
         for h in two:
-            an[h].append(send("y", an[h][-1]))
-            jn[h].append(send("z", jn[h][-1]))
+            x, v = lax.optimization_barrier((an[h][-1], jn[h][-1]))
+            an[h].append(send("y", x))
+            jn[h].append(send("z", v))
     rest = flat(an, range(4))
     rest_other = send("core", jnp.concatenate(rest, 0), jn[0][3], jn[1][3])
     both = [columns(0, j), columns(1, jn)]

time: 137 us -> 133 us (0.971)
  starting transfers between devices: 63.4 us -> 51.6 us
  local copies, waits for them, and re-layouts: 18.5 us -> 22.2 us
  Pallas kernels: 31 us -> 32.7 us
  waiting for transfers between devices: 22.2 us -> 23.6 us
    ppermute x30, starting transfers between devices: 63.4 us -> 51.6 us  [send(): return lax.ppermute(after(block, *earlier), axis, pairs)]
    unnamed x84 -> x72, local copies, waits for them, and re-layouts: 14.6 us -> 18.4 us
    pallas_call x1, Pallas kernels: 0.82 us -> 2.57 us  [scale(): pl.pallas_call(kernel, out_shape=[jax.ShapeDtypeStruct((PIECE, pairs), jn...]
    reshape x2 -> x0, local copies, waits for them, and re-layouts: 1.41 us -> none  [table(): return jnp.pad(energy, (0, padded - energy.shape[0])).reshape(-1, LANES)]
  transfers between devices with their start and end apart: 30 -> 30, of which waited for: 8 -> 10; matrix products, arithmetic and copies ran while one was open for 11% -> 16% of each run, Pallas kernels for 14% -> 15%
where the time goes in v4:
time: 133 us; the launch traced here: 132 us
  starting transfers between devices  51.6 us (39%)
  Pallas kernels  32.7 us (25%)
  waiting for transfers between devices  23.6 us (18%)
  local copies, waits for them, and re-layouts  22.2 us (17%)
  other arithmetic  1.34 us (1%)
    ppermute x30, starting transfers between devices, send(): return lax.ppermute(after(block, *earlier), axis, pairs)  51.6 us
    pallas_call x2, Pallas kernels, multiply(): pl.pallas_call(kernel, out_shape=jax.ShapeDtypeStruct((N_COL * LANES, 2,...  30.2 us
    ppermute x30, waiting for transfers between devices, send(): return lax.ppermute(after(block, *earlier), axis, pairs)  23.6 us
    unnamed x72, local copies, waits for them, and re-layouts  18.4 us
  transfers between devices with their start and end apart: 30, of which 10 were waited for; matrix products, arithmetic and copies ran while one was open for 16% of the time, Pallas kernels for 15%

profile of v4, /device:TPU:1, one launch (start us, length us, event | category | flops | bytes accessed | tf_op | source)
XLA Modules:
  0.0 132.5 jit_solution(11069923301130118507)
XLA Ops:
  2.0 2.6 %shard_map.64 = (bf16[64,4096]{1,0:T(8,128)(2,1)}, bf16[64,4096]{1,0:T(8,128)(2,1)}) custom-call(f32[1]{0:T(128)S(6)} %copy.24.freq, s32[32,128]{1,0:T(8,128)} %bitcast.49, s32[32,128]{1,0:T(8,128)} %bitcast.50, f32[40,128]{1,0:T(8,128)} %fusion.refs_2_, bf16[128,4096]{1,0:T(8,128)(2,1)} %refs_3_.1), custom_call_target="tpu_custom_call" | custom-call | tf_op jit(solution)/shard_map/pallas_call | solution.py:80
  4.6 3.6 %collective-permute-start.2 = (bf16[64,4096]{1,0:T(8,128)(2,1)}, bf16[64,4096]{1,0:T(8,128)(2,1)S(1)}, u32[]{:S(2)}, u32[]{:S(2)}) collective-permute-start(bf16[64,4096]{1,0:T(8,128)(2,1)} %get-tuple-element.35.refs_0_), channel_id=1, source_target_pairs={{0,2},{1,7},{2,4},{3,1},{4,6},{5,3},{6,0},{7,5},{8,10},{9,15},{10,... | collective-permute-start | bytes 1572872 | tf_op jit(solution)/shard_map/ppermute | solution.py:36
  10.7 3.8 %collective-permute-start.3 = (bf16[64,4096]{1,0:T(8,128)(2,1)S(1)}, bf16[64,4096]{1,0:T(8,128)(2,1)S(1)}, u32[]{:S(2)}, u32[]{:S(2)}) collective-permute-start(bf16[64,4096]{1,0:T(8,128)(2,1)S(1)} %get-tuple-element.66.refs_17_.refs_1_), channel_id=1, source_target_pairs={{0,16},{16,32},{32,48},{48,0},{64,80},{80,96},{96,112},{112,64},{1... | collective-permute-start | bytes 1572872 | tf_op jit(solution)/shard_map/ppermute | solution.py:36
  14.6 2.5 %collective-permute-start.1 = (bf16[64,4096]{1,0:T(8,128)(2,1)S(1)}, bf16[64,4096]{1,0:T(8,128)(2,1)S(1)}, u32[]{:S(2)}, u32[]{:S(2)}) collective-permute-start(bf16[64,4096]{1,0:T(8,128)(2,1)S(1)} %get-tuple-element.66.refs_17_.refs_1_), channel_id=1, source_target_pairs={{0,64},{16,80},{32,96},{48,112},{64,0},{80,16},{96,32},{112,48},{1... | collective-permute-start | bytes 1572872 | tf_op jit(solution)/shard_map/ppermute | solution.py:36
  19.2 1.9 %constant_dynamic-update-slice_fusion.15 = bf16[512,4096]{1,0:T(8,128)(2,1)} fusion(bf16[64,4096]{1,0:T(8,128)(2,1)} %get-tuple-element.35.refs_0_), kind=kLoop, calls=%fused_computation.15 | loop fusion | bytes 1048576
  23.6 3.0 %collective-permute-start.4 = (bf16[64,4096]{1,0:T(8,128)(2,1)}, bf16[64,4096]{1,0:T(8,128)(2,1)S(1)}, u32[]{:S(2)}, u32[]{:S(2)}) collective-permute-start(bf16[64,4096]{1,0:T(8,128)(2,1)} %copy-done.17), channel_id=1, source_target_pairs={{0,2},{1,7},{2,4},{3,1},{4,6},{5,3},{6,0},{7,5},{8,10},{9,15},{10,... | collective-permute-start | bytes 1572872 | tf_op jit(solution)/shard_map/ppermute | solution.py:36
  28.4 3.4 %collective-permute-start.5 = (bf16[64,4096]{1,0:T(8,128)(2,1)S(1)}, bf16[64,4096]{1,0:T(8,128)(2,1)S(1)}, u32[]{:S(2)}, u32[]{:S(2)}) collective-permute-start(bf16[64,4096]{1,0:T(8,128)(2,1)S(1)} %collective-permute-done.3.refs_19_.refs_3_), channel_id=1, source_target_pairs={{0,16},{16,32},{32,48},{48,0},{64,80},{80,96},{96,112},{112,64},{1... | collective-permute-start | bytes 1572872 | tf_op jit(solution)/shard_map/ppermute | solution.py:36
  31.8 3.9 %collective-permute-done.1.refs_25_.refs_9_ = bf16[64,4096]{1,0:T(8,128)(2,1)S(1)} collective-permute-done((bf16[64,4096]{1,0:T(8,128)(2,1)S(1)}, bf16[64,4096]{1,0:T(8,128)(2,1)S(1)}, u32[]{:S(2)}, u32[]{:S(2)}) %collective-permute-start.1) | collective-permute-done | bytes 524320 | tf_op jit(solution)/shard_map/ppermute | solution.py:36
  35.8 2.1 %constant_dynamic-update-slice_fusion.13 = bf16[512,4096]{1,0:T(8,128)(2,1)} fusion(bf16[512,4096]{1,0:T(8,128)(2,1)} %constant_dynamic-update-slice_fusion.14, bf16[64,4096]{1,0:T(8,128)(2,1)} %copy-done.17), kind=kLoop, calls=%fused_computation.13 | loop fusion | bytes 1048576
  40.9 2.6 %collective-permute-done.13.refs_22_.refs_6_ = bf16[64,4096]{1,0:T(8,128)(2,1)S(1)} collective-permute-done((bf16[64,4096]{1,0:T(8,128)(2,1)S(1)}, bf16[64,4096]{1,0:T(8,128)(2,1)S(1)}, u32[]{:S(2)}, u32[]{:S(2)}) %collective-permute-start.13) | collective-permute-done | bytes 524320 | tf_op jit(solution)/shard_map/ppermute | solution.py:36
  43.5 3.1 %collective-permute-start.15 = (bf16[64,4096]{1,0:T(8,128)(2,1)S(1)}, bf16[64,4096]{1,0:T(8,128)(2,1)S(1)}, u32[]{:S(2)}, u32[]{:S(2)}) collective-permute-start(bf16[64,4096]{1,0:T(8,128)(2,1)S(1)} %collective-permute-done.13.refs_22_.refs_6_), channel_id=1, source_target_pairs={{0,16},{16,32},{32,48},{48,0},{64,80},{80,96},{96,112},{112,64},{1... | collective-permute-start | bytes 1572872 | tf_op jit(solution)/shard_map/ppermute | solution.py:36
  46.7 2.2 %collective-permute-done.8.refs_10_ = bf16[64,4096]{1,0:T(8,128)(2,1)S(1)} collective-permute-done((bf16[64,4096]{1,0:T(8,128)(2,1)S(1)}, bf16[64,4096]{1,0:T(8,128)(2,1)S(1)}, u32[]{:S(2)}, u32[]{:S(2)}) %collective-permute-start.8) | collective-permute-done | bytes 524320 | tf_op jit(solution)/shard_map/ppermute | solution.py:36
  48.9 3.8 %collective-permute-start.7 = (bf16[64,4096]{1,0:T(8,128)(2,1)S(1)}, bf16[64,4096]{1,0:T(8,128)(2,1)S(1)}, u32[]{:S(2)}, u32[]{:S(2)}) collective-permute-start(bf16[64,4096]{1,0:T(8,128)(2,1)S(1)} %collective-permute-done.5.refs_21_.refs_5_), channel_id=1, source_target_pairs={{0,16},{16,32},{32,48},{48,0},{64,80},{80,96},{96,112},{112,64},{1... | collective-permute-start | bytes 1572872 | tf_op jit(solution)/shard_map/ppermute | solution.py:36
  54.3 5.7 %collective-permute-done.9.refs_26_.refs_10_ = bf16[64,4096]{1,0:T(8,128)(2,1)S(1)} collective-permute-done((bf16[64,4096]{1,0:T(8,128)(2,1)S(1)}, bf16[64,4096]{1,0:T(8,128)(2,1)S(1)}, u32[]{:S(2)}, u32[]{:S(2)}) %collective-permute-start.9) | collective-permute-done | bytes 524320 | tf_op jit(solution)/shard_map/ppermute | solution.py:36
  60.1 3.8 %collective-permute-start.20 = (bf16[64,4096]{1,0:T(8,128)(2,1)S(1)}, bf16[64,4096]{1,0:T(8,128)(2,1)S(1)}, u32[]{:S(2)}, u32[]{:S(2)}) collective-permute-start(bf16[64,4096]{1,0:T(8,128)(2,1)S(1)} %collective-permute-done.9.refs_26_.refs_10_), channel_id=1, source_target_pairs={{0,16},{16,32},{32,48},{48,0},{64,80},{80,96},{96,112},{112,64},{1... | collective-permute-start | bytes 1572872 | tf_op jit(solution)/shard_map/ppermute | solution.py:36
  64.0 2.2 %constant_dynamic-update-slice_fusion.7 = bf16[512,4096]{1,0:T(8,128)(2,1)} fusion(bf16[64,4096]{1,0:T(8,128)(2,1)} %collective-permute-done.refs_9_), kind=kLoop, calls=%fused_computation.7 | loop fusion | bytes 1048576
  70.1 3.0 %collective-permute-start.21 = (bf16[64,4096]{1,0:T(8,128)(2,1)S(1)}, bf16[64,4096]{1,0:T(8,128)(2,1)S(1)}, u32[]{:S(2)}, u32[]{:S(2)}) collective-permute-start(bf16[64,4096]{1,0:T(8,128)(2,1)S(1)} %collective-permute-done.17.refs_12_), channel_id=1, source_target_pairs={{0,2},{1,7},{2,4},{3,1},{4,6},{5,3},{6,0},{7,5},{8,10},{9,15},{10,... | collective-permute-start | bytes 1572872 | tf_op jit(solution)/shard_map/ppermute | solution.py:36
  76.0 3.1 %collective-permute-start.22 = (bf16[64,4096]{1,0:T(8,128)(2,1)S(1)}, bf16[64,4096]{1,0:T(8,128)(2,1)S(1)}, u32[]{:S(2)}, u32[]{:S(2)}) collective-permute-start(bf16[64,4096]{1,0:T(8,128)(2,1)S(1)} %collective-permute-done.18.refs_27_.refs_11_), channel_id=1, source_target_pairs={{0,16},{16,32},{32,48},{48,0},{64,80},{80,96},{96,112},{112,64},{1... | collective-permute-start | bytes 1572872 | tf_op jit(solution)/shard_map/ppermute | solution.py:36
  83.1 2.0 %collective-permute-start.27 = (bf16[64,4096]{1,0:T(8,128)(2,1)S(1)}, bf16[64,4096]{1,0:T(8,128)(2,1)S(1)}, u32[]{:S(2)}, u32[]{:S(2)}) collective-permute-start(bf16[64,4096]{1,0:T(8,128)(2,1)S(1)} %collective-permute-done.24.refs_30_.refs_14_), channel_id=1, source_target_pairs={{0,16},{16,32},{32,48},{48,0},{64,80},{80,96},{96,112},{112,64},{1... | collective-permute-start | bytes 1572872 | tf_op jit(solution)/shard_map/ppermute | solution.py:36
  88.7 2.0 %collective-permute-start.26 = (bf16[64,4096]{1,0:T(8,128)(2,1)S(1)}, bf16[64,4096]{1,0:T(8,128)(2,1)S(1)}, u32[]{:S(2)}, u32[]{:S(2)}) collective-permute-start(bf16[64,4096]{1,0:T(8,128)(2,1)S(1)} %collective-permute-done.22.refs_29_.refs_13_), channel_id=1, source_target_pairs={{0,16},{16,32},{32,48},{48,0},{64,80},{80,96},{96,112},{112,64},{1... | collective-permute-start | bytes 1572872 | tf_op jit(solution)/shard_map/ppermute | solution.py:36
  92.3 4.9 %collective-permute-done.23.refs_15_ = bf16[64,4096]{1,0:T(8,128)(2,1)S(1)} collective-permute-done((bf16[64,4096]{1,0:T(8,128)(2,1)S(1)}, bf16[64,4096]{1,0:T(8,128)(2,1)S(1)}, u32[]{:S(2)}, u32[]{:S(2)}) %collective-permute-start.23) | collective-permute-done | bytes 524320 | tf_op jit(solution)/shard_map/ppermute | solution.py:36
  99.2 2.9 %collective-permute-start.28 = (bf16[512,4096]{1,0:T(8,128)(2,1)}, bf16[512,4096]{1,0:T(8,128)(2,1)}, u32[]{:S(2)}, u32[]{:S(2)}) collective-permute-start(bf16[512,4096]{1,0:T(8,128)(2,1)} %constant_dynamic-update-slice_fusion), channel_id=1, source_target_pairs={{0,1},{1,0},{2,3},{3,2},{4,5},{5,4},{6,7},{7,6},{8,9},{9,8},{10,11... | collective-permute-start | bytes 12582920 | tf_op jit(solution)/shard_map/ppermute | solution.py:36
  102.1 19.7 %shard_map.65.refs_17_ = f32[2048,2,4,128]{3,2,1,0:T(4,128)} custom-call(s32[42]{0:T(128)} %stack.171.number, bf16[64,4096]{1,0:T(8,128)(2,1)} %get-tuple-element.35.refs_0_, bf16[64,4096]{1,0:T(8,128)(2,1)} %get-tuple-element.42.refs_1_, bf16[64,4096]{1,0:T(8,128)(2,1)} %copy-done.17, bf16[64,4096]{1,0:T(8,128)(2,1)} %collective-permute-done.10.refs_3_, ...), custom_call_target="tpu_custom_call" | custom-call | flops 12884901888 | bytes 16777216 | tf_op jit(solution)/shard_map/pallas_call | solution.py:169
  121.9 10.4 %shard_map.66 = f32[2048,2,4,128]{3,2,1,0:T(4,128)} custom-call(s32[42]{0:T(128)} %stack.171.number, bf16[512,4096]{1,0:T(8,128)(2,1)} %collective-permute-done.28.refs_0_, bf16[64,4096]{1,0:T(8,128)(2,1)} %copy-done.1, bf16[64,4096]{1,0:T(8,128)(2,1)} %copy-done, bf16[64,4096]{1,0:T(8,128)(2,1)} %copy-done.2, ...), custom_call_target="tpu_custom_call", output_to_operand_aliasing={{}: (18, {})} | custom-call | flops 4294967296 | bytes 16777216 | tf_op jit(solution)/shard_map/pallas_call | solution.py:169
  (116 shorter events, 33.2 us)
Async XLA Ops:
  4.6 12.9 %collective-permute-start.2 = (bf16[64,4096]{1,0:T(8,128)(2,1)}, bf16[64,4096]{1,0:T(8,128)(2,1)S(1)}, u32[]{:S(2)}, u32[]{:S(2)}) collective-permute-start(bf16[64,4096]{1,0:T(8,128)(2,1)} %get-tuple-element.35.refs_0_), channel_id=1, source_target_pairs={{0,2},{1,7},{2,4},{3,1},{4,6},{5,3},{6,0},{7,5},{8,10},{9,15},{10,... | collective-permute-start | bytes 1572872 | tf_op jit(solution)/shard_map/ppermute | solution.py:36
  8.2 23.6 %collective-permute-start = (bf16[64,4096]{1,0:T(8,128)(2,1)}, bf16[64,4096]{1,0:T(8,128)(2,1)}, u32[]{:S(2)}, u32[]{:S(2)}) collective-permute-start(bf16[64,4096]{1,0:T(8,128)(2,1)} %get-tuple-element.35.refs_0_), channel_id=1, source_target_pairs={{0,8},{1,9},{2,10},{3,11},{4,12},{5,13},{6,14},{7,15},{8,0},{9,1},... | collective-permute-start | bytes 1572872 | tf_op jit(solution)/shard_map/ppermute | solution.py:36
  10.7 12.9 %collective-permute-start.3 = (bf16[64,4096]{1,0:T(8,128)(2,1)S(1)}, bf16[64,4096]{1,0:T(8,128)(2,1)S(1)}, u32[]{:S(2)}, u32[]{:S(2)}) collective-permute-start(bf16[64,4096]{1,0:T(8,128)(2,1)S(1)} %get-tuple-element.66.refs_17_.refs_1_), channel_id=1, source_target_pairs={{0,16},{16,32},{32,48},{48,0},{64,80},{80,96},{96,112},{112,64},{1... | collective-permute-start | bytes 1572872 | tf_op jit(solution)/shard_map/ppermute | solution.py:36
  14.6 21.2 %collective-permute-start.1 = (bf16[64,4096]{1,0:T(8,128)(2,1)S(1)}, bf16[64,4096]{1,0:T(8,128)(2,1)S(1)}, u32[]{:S(2)}, u32[]{:S(2)}) collective-permute-start(bf16[64,4096]{1,0:T(8,128)(2,1)S(1)} %get-tuple-element.66.refs_17_.refs_1_), channel_id=1, source_target_pairs={{0,64},{16,80},{32,96},{48,112},{64,0},{80,16},{96,32},{112,48},{1... | collective-permute-start | bytes 1572872 | tf_op jit(solution)/shard_map/ppermute | solution.py:36
  23.6 16.1 %collective-permute-start.4 = (bf16[64,4096]{1,0:T(8,128)(2,1)}, bf16[64,4096]{1,0:T(8,128)(2,1)S(1)}, u32[]{:S(2)}, u32[]{:S(2)}) collective-permute-start(bf16[64,4096]{1,0:T(8,128)(2,1)} %copy-done.17), channel_id=1, source_target_pairs={{0,2},{1,7},{2,4},{3,1},{4,6},{5,3},{6,0},{7,5},{8,10},{9,15},{10,... | collective-permute-start | bytes 1572872 | tf_op jit(solution)/shard_map/ppermute | solution.py:36
  26.7 14.2 %collective-permute-start.12 = (bf16[64,4096]{1,0:T(8,128)(2,1)}, bf16[64,4096]{1,0:T(8,128)(2,1)S(1)}, u32[]{:S(2)}, u32[]{:S(2)}) collective-permute-start(bf16[64,4096]{1,0:T(8,128)(2,1)} %collective-permute-done.10.refs_3_), channel_id=1, source_target_pairs={{0,2},{1,7},{2,4},{3,1},{4,6},{5,3},{6,0},{7,5},{8,10},{9,15},{10,... | collective-permute-start | bytes 1572872 | tf_op jit(solution)/shard_map/ppermute | solution.py:36
  28.4 12.5 %collective-permute-start.5 = (bf16[64,4096]{1,0:T(8,128)(2,1)S(1)}, bf16[64,4096]{1,0:T(8,128)(2,1)S(1)}, u32[]{:S(2)}, u32[]{:S(2)}) collective-permute-start(bf16[64,4096]{1,0:T(8,128)(2,1)S(1)} %collective-permute-done.3.refs_19_.refs_3_), channel_id=1, source_target_pairs={{0,16},{16,32},{32,48},{48,0},{64,80},{80,96},{96,112},{112,64},{1... | collective-permute-start | bytes 1572872 | tf_op jit(solution)/shard_map/ppermute | solution.py:36
  31.8 11.7 %collective-permute-start.13 = (bf16[64,4096]{1,0:T(8,128)(2,1)S(1)}, bf16[64,4096]{1,0:T(8,128)(2,1)S(1)}, u32[]{:S(2)}, u32[]{:S(2)}) collective-permute-start(bf16[64,4096]{1,0:T(8,128)(2,1)S(1)} %collective-permute-done.11.refs_20_.refs_4_), channel_id=1, source_target_pairs={{0,16},{16,32},{32,48},{48,0},{64,80},{80,96},{96,112},{112,64},{1... | collective-permute-start | bytes 1572872 | tf_op jit(solution)/shard_map/ppermute | solution.py:36
  35.8 13.1 %collective-permute-start.8 = (bf16[64,4096]{1,0:T(8,128)(2,1)S(1)}, bf16[64,4096]{1,0:T(8,128)(2,1)S(1)}, u32[]{:S(2)}, u32[]{:S(2)}) collective-permute-start(bf16[64,4096]{1,0:T(8,128)(2,1)S(1)} %copy-done.16), channel_id=1, source_target_pairs={{0,8},{1,9},{2,10},{3,11},{4,12},{5,13},{6,14},{7,15},{8,0},{9,1},... | collective-permute-start | bytes 1572872 | tf_op jit(solution)/shard_map/ppermute | solution.py:36
  39.7 20.3 %collective-permute-start.9 = (bf16[64,4096]{1,0:T(8,128)(2,1)S(1)}, bf16[64,4096]{1,0:T(8,128)(2,1)S(1)}, u32[]{:S(2)}, u32[]{:S(2)}) collective-permute-start(bf16[64,4096]{1,0:T(8,128)(2,1)S(1)} %get-tuple-element.43.refs_18_.refs_2_), channel_id=1, source_target_pairs={{0,64},{16,80},{32,96},{48,112},{64,0},{80,16},{96,32},{112,48},{1... | collective-permute-start | bytes 1572872 | tf_op jit(solution)/shard_map/ppermute | solution.py:36
  40.9 23.1 %collective-permute-start.6 = (bf16[64,4096]{1,0:T(8,128)(2,1)S(1)}, bf16[64,4096]{1,0:T(8,128)(2,1)S(1)}, u32[]{:S(2)}, u32[]{:S(2)}) collective-permute-start(bf16[64,4096]{1,0:T(8,128)(2,1)S(1)} %collective-permute-done.4.refs_4_), channel_id=1, source_target_pairs={{0,2},{1,7},{2,4},{3,1},{4,6},{5,3},{6,0},{7,5},{8,10},{9,15},{10,... | collective-permute-start | bytes 1572872 | tf_op jit(solution)/shard_map/ppermute | solution.py:36
  43.5 16.5 %collective-permute-start.14 = (bf16[64,4096]{1,0:T(8,128)(2,1)S(1)}, bf16[64,4096]{1,0:T(8,128)(2,1)S(1)}, u32[]{:S(2)}, u32[]{:S(2)}) collective-permute-start(bf16[64,4096]{1,0:T(8,128)(2,1)S(1)} %collective-permute-done.12.refs_5_), channel_id=1, source_target_pairs={{0,2},{1,7},{2,4},{3,1},{4,6},{5,3},{6,0},{7,5},{8,10},{9,15},{10,... | collective-permute-start | bytes 1572872 | tf_op jit(solution)/shard_map/ppermute | solution.py:36
  43.5 16.5 %collective-permute-start.15 = (bf16[64,4096]{1,0:T(8,128)(2,1)S(1)}, bf16[64,4096]{1,0:T(8,128)(2,1)S(1)}, u32[]{:S(2)}, u32[]{:S(2)}) collective-permute-start(bf16[64,4096]{1,0:T(8,128)(2,1)S(1)} %collective-permute-done.13.refs_22_.refs_6_), channel_id=1, source_target_pairs={{0,16},{16,32},{32,48},{48,0},{64,80},{80,96},{96,112},{112,64},{1... | collective-permute-start | bytes 1572872 | tf_op jit(solution)/shard_map/ppermute | solution.py:36
  48.9 15.1 %collective-permute-start.7 = (bf16[64,4096]{1,0:T(8,128)(2,1)S(1)}, bf16[64,4096]{1,0:T(8,128)(2,1)S(1)}, u32[]{:S(2)}, u32[]{:S(2)}) collective-permute-start(bf16[64,4096]{1,0:T(8,128)(2,1)S(1)} %collective-permute-done.5.refs_21_.refs_5_), channel_id=1, source_target_pairs={{0,16},{16,32},{32,48},{48,0},{64,80},{80,96},{96,112},{112,64},{1... | collective-permute-start | bytes 1572872 | tf_op jit(solution)/shard_map/ppermute | solution.py:36
  60.0 10.0 %collective-permute-start.17 = (bf16[64,4096]{1,0:T(8,128)(2,1)S(1)}, bf16[64,4096]{1,0:T(8,128)(2,1)S(1)}, u32[]{:S(2)}, u32[]{:S(2)}) collective-permute-start(bf16[64,4096]{1,0:T(8,128)(2,1)S(1)} %collective-permute-done.8.refs_10_), channel_id=1, source_target_pairs={{0,2},{1,7},{2,4},{3,1},{4,6},{5,3},{6,0},{7,5},{8,10},{9,15},{10,... | collective-permute-start | bytes 1572872 | tf_op jit(solution)/shard_map/ppermute | solution.py:36
  68.0 34.0 %collective-permute-start.29 = (bf16[512,4096]{1,0:T(8,128)(2,1)}, bf16[512,4096]{1,0:T(8,128)(2,1)}, u32[]{:S(2)}, u32[]{:S(2)}) collective-permute-start(bf16[512,4096]{1,0:T(8,128)(2,1)} %constant_dynamic-update-slice_fusion.8), channel_id=1, source_target_pairs={{0,1},{1,0},{2,3},{3,2},{4,5},{5,4},{6,7},{7,6},{8,9},{9,8},{10,11... | collective-permute-start | bytes 12582920 | tf_op jit(solution)/shard_map/ppermute | solution.py:36
  70.1 10.7 %collective-permute-start.21 = (bf16[64,4096]{1,0:T(8,128)(2,1)S(1)}, bf16[64,4096]{1,0:T(8,128)(2,1)S(1)}, u32[]{:S(2)}, u32[]{:S(2)}) collective-permute-start(bf16[64,4096]{1,0:T(8,128)(2,1)S(1)} %collective-permute-done.17.refs_12_), channel_id=1, source_target_pairs={{0,2},{1,7},{2,4},{3,1},{4,6},{5,3},{6,0},{7,5},{8,10},{9,15},{10,... | collective-permute-start | bytes 1572872 | tf_op jit(solution)/shard_map/ppermute | solution.py:36
  75.7 10.3 %collective-permute-start.19 = (bf16[64,4096]{1,0:T(8,128)(2,1)S(1)}, bf16[64,4096]{1,0:T(8,128)(2,1)S(1)}, u32[]{:S(2)}, u32[]{:S(2)}) collective-permute-start(bf16[64,4096]{1,0:T(8,128)(2,1)S(1)} %collective-permute-done.16.refs_11_), channel_id=1, source_target_pairs={{0,2},{1,7},{2,4},{3,1},{4,6},{5,3},{6,0},{7,5},{8,10},{9,15},{10,... | collective-permute-start | bytes 1572872 | tf_op jit(solution)/shard_map/ppermute | solution.py:36
  76.0 11.0 %collective-permute-start.22 = (bf16[64,4096]{1,0:T(8,128)(2,1)S(1)}, bf16[64,4096]{1,0:T(8,128)(2,1)S(1)}, u32[]{:S(2)}, u32[]{:S(2)}) collective-permute-start(bf16[64,4096]{1,0:T(8,128)(2,1)S(1)} %collective-permute-done.18.refs_27_.refs_11_), channel_id=1, source_target_pairs={{0,16},{16,32},{32,48},{48,0},{64,80},{80,96},{96,112},{112,64},{1... | collective-permute-start | bytes 1572872 | tf_op jit(solution)/shard_map/ppermute | solution.py:36
  81.4 16.7 %collective-permute-start.25 = (bf16[64,4096]{1,0:T(8,128)(2,1)S(1)}, bf16[64,4096]{1,0:T(8,128)(2,1)S(1)}, u32[]{:S(2)}, u32[]{:S(2)}) collective-permute-start(bf16[64,4096]{1,0:T(8,128)(2,1)S(1)} %collective-permute-done.21.refs_14_), channel_id=1, source_target_pairs={{0,2},{1,7},{2,4},{3,1},{4,6},{5,3},{6,0},{7,5},{8,10},{9,15},{10,... | collective-permute-start | bytes 1572872 | tf_op jit(solution)/shard_map/ppermute | solution.py:36
  83.1 16.0 %collective-permute-start.27 = (bf16[64,4096]{1,0:T(8,128)(2,1)S(1)}, bf16[64,4096]{1,0:T(8,128)(2,1)S(1)}, u32[]{:S(2)}, u32[]{:S(2)}) collective-permute-start(bf16[64,4096]{1,0:T(8,128)(2,1)S(1)} %collective-permute-done.24.refs_30_.refs_14_), channel_id=1, source_target_pairs={{0,16},{16,32},{32,48},{48,0},{64,80},{80,96},{96,112},{112,64},{1... | collective-permute-start | bytes 1572872 | tf_op jit(solution)/shard_map/ppermute | solution.py:36
  87.1 10.2 %collective-permute-start.23 = (bf16[64,4096]{1,0:T(8,128)(2,1)S(1)}, bf16[64,4096]{1,0:T(8,128)(2,1)S(1)}, u32[]{:S(2)}, u32[]{:S(2)}) collective-permute-start(bf16[64,4096]{1,0:T(8,128)(2,1)S(1)} %collective-permute-done.19.refs_13_), channel_id=1, source_target_pairs={{0,2},{1,7},{2,4},{3,1},{4,6},{5,3},{6,0},{7,5},{8,10},{9,15},{10,... | collective-permute-start | bytes 1572872 | tf_op jit(solution)/shard_map/ppermute | solution.py:36
  88.7 10.4 %collective-permute-start.26 = (bf16[64,4096]{1,0:T(8,128)(2,1)S(1)}, bf16[64,4096]{1,0:T(8,128)(2,1)S(1)}, u32[]{:S(2)}, u32[]{:S(2)}) collective-permute-start(bf16[64,4096]{1,0:T(8,128)(2,1)S(1)} %collective-permute-done.22.refs_29_.refs_13_), channel_id=1, source_target_pairs={{0,16},{16,32},{32,48},{48,0},{64,80},{80,96},{96,112},{112,64},{1... | collective-permute-start | bytes 1572872 | tf_op jit(solution)/shard_map/ppermute | solution.py:36
  99.2 22.7 %collective-permute-start.28 = (bf16[512,4096]{1,0:T(8,128)(2,1)}, bf16[512,4096]{1,0:T(8,128)(2,1)}, u32[]{:S(2)}, u32[]{:S(2)}) collective-permute-start(bf16[512,4096]{1,0:T(8,128)(2,1)} %constant_dynamic-update-slice_fusion), channel_id=1, source_target_pairs={{0,1},{1,0},{2,3},{3,2},{4,5},{5,4},{6,7},{7,6},{8,9},{9,8},{10,11... | collective-permute-start | bytes 12582920 | tf_op jit(solution)/shard_map/ppermute | solution.py:36
  (35 other events, 840.2 us)

commit v5 on v4

--- a/solution.py
+++ b/solution.py
@@ -136,7 +136,7 @@
                     c.wait()
                 for c in sum(j_loads[1:], []):
                     c.start()
-            if t + 1 < len(tiles):
+            if t and t + 1 < len(tiles):
                 for c in a_load(t + 1):
                     c.start()
             m = len(tile) * PIECE
@@ -144,6 +144,9 @@
                 if t == 0 and g > 0:
                     for c in j_loads[g]:
                         c.wait()
+                    if g == n_g - 1 and len(tiles) > 1:
+                        for c in a_load(1):
+                            c.start()
                 slot = step % 2
                 step += 1
                 for c in pending[slot]:

time: 133 us -> 133 us (level)
  no operation moved by 1% of the time
where the time goes in v5:
time: 133 us
  starting transfers between devices  51.6 us (39%)
  Pallas kernels  32.9 us (25%)
  waiting for transfers between devices  23.6 us (18%)
  local copies, waits for them, and re-layouts  22.2 us (17%)
  other arithmetic  1.34 us (1%)
    ppermute x30, starting transfers between devices, send(): return lax.ppermute(after(block, *earlier), axis, pairs)  51.6 us
    pallas_call x2, Pallas kernels, multiply(): pl.pallas_call(kernel, out_shape=jax.ShapeDtypeStruct((N_COL * LANES, 2,...  30.3 us
    ppermute x30, waiting for transfers between devices, send(): return lax.ppermute(after(block, *earlier), axis, pairs)  23.6 us
    unnamed x72, local copies, waits for them, and re-layouts  18.4 us
  transfers between devices with their start and end apart: 30, of which 10 were waited for; matrix products, arithmetic and copies ran while one was open for 16% of the time, Pallas kernels for 15%

profile of v5, /device:TPU:1, one launch (start us, length us, event | category | flops | bytes accessed | tf_op | source)
XLA Modules:
  0.0 132.6 jit_solution(11598508851901697712)
XLA Ops:
  2.0 2.6 %shard_map.64 = (bf16[64,4096]{1,0:T(8,128)(2,1)}, bf16[64,4096]{1,0:T(8,128)(2,1)}) custom-call(f32[1]{0:T(128)S(6)} %copy.24.freq, s32[32,128]{1,0:T(8,128)} %bitcast.49, s32[32,128]{1,0:T(8,128)} %bitcast.50, f32[40,128]{1,0:T(8,128)} %fusion.refs_2_, bf16[128,4096]{1,0:T(8,128)(2,1)} %refs_3_.1), custom_call_target="tpu_custom_call" | custom-call | tf_op jit(solution)/shard_map/pallas_call | solution.py:80
  4.6 3.6 %collective-permute-start.2 = (bf16[64,4096]{1,0:T(8,128)(2,1)}, bf16[64,4096]{1,0:T(8,128)(2,1)S(1)}, u32[]{:S(2)}, u32[]{:S(2)}) collective-permute-start(bf16[64,4096]{1,0:T(8,128)(2,1)} %get-tuple-element.35.refs_0_), channel_id=1, source_target_pairs={{0,2},{1,7},{2,4},{3,1},{4,6},{5,3},{6,0},{7,5},{8,10},{9,15},{10,... | collective-permute-start | bytes 1572872 | tf_op jit(solution)/shard_map/ppermute | solution.py:36
  10.7 3.8 %collective-permute-start.3 = (bf16[64,4096]{1,0:T(8,128)(2,1)S(1)}, bf16[64,4096]{1,0:T(8,128)(2,1)S(1)}, u32[]{:S(2)}, u32[]{:S(2)}) collective-permute-start(bf16[64,4096]{1,0:T(8,128)(2,1)S(1)} %get-tuple-element.66.refs_17_.refs_1_), channel_id=1, source_target_pairs={{0,16},{16,32},{32,48},{48,0},{64,80},{80,96},{96,112},{112,64},{1... | collective-permute-start | bytes 1572872 | tf_op jit(solution)/shard_map/ppermute | solution.py:36
  14.6 2.5 %collective-permute-start.1 = (bf16[64,4096]{1,0:T(8,128)(2,1)S(1)}, bf16[64,4096]{1,0:T(8,128)(2,1)S(1)}, u32[]{:S(2)}, u32[]{:S(2)}) collective-permute-start(bf16[64,4096]{1,0:T(8,128)(2,1)S(1)} %get-tuple-element.66.refs_17_.refs_1_), channel_id=1, source_target_pairs={{0,64},{16,80},{32,96},{48,112},{64,0},{80,16},{96,32},{112,48},{1... | collective-permute-start | bytes 1572872 | tf_op jit(solution)/shard_map/ppermute | solution.py:36
  19.2 1.9 %constant_dynamic-update-slice_fusion.15 = bf16[512,4096]{1,0:T(8,128)(2,1)} fusion(bf16[64,4096]{1,0:T(8,128)(2,1)} %get-tuple-element.35.refs_0_), kind=kLoop, calls=%fused_computation.15 | loop fusion | bytes 1048576
  23.6 3.0 %collective-permute-start.4 = (bf16[64,4096]{1,0:T(8,128)(2,1)}, bf16[64,4096]{1,0:T(8,128)(2,1)S(1)}, u32[]{:S(2)}, u32[]{:S(2)}) collective-permute-start(bf16[64,4096]{1,0:T(8,128)(2,1)} %copy-done.17), channel_id=1, source_target_pairs={{0,2},{1,7},{2,4},{3,1},{4,6},{5,3},{6,0},{7,5},{8,10},{9,15},{10,... | collective-permute-start | bytes 1572872 | tf_op jit(solution)/shard_map/ppermute | solution.py:36
  28.4 3.4 %collective-permute-start.5 = (bf16[64,4096]{1,0:T(8,128)(2,1)S(1)}, bf16[64,4096]{1,0:T(8,128)(2,1)S(1)}, u32[]{:S(2)}, u32[]{:S(2)}) collective-permute-start(bf16[64,4096]{1,0:T(8,128)(2,1)S(1)} %collective-permute-done.3.refs_19_.refs_3_), channel_id=1, source_target_pairs={{0,16},{16,32},{32,48},{48,0},{64,80},{80,96},{96,112},{112,64},{1... | collective-permute-start | bytes 1572872 | tf_op jit(solution)/shard_map/ppermute | solution.py:36
  31.8 3.9 %collective-permute-done.1.refs_25_.refs_9_ = bf16[64,4096]{1,0:T(8,128)(2,1)S(1)} collective-permute-done((bf16[64,4096]{1,0:T(8,128)(2,1)S(1)}, bf16[64,4096]{1,0:T(8,128)(2,1)S(1)}, u32[]{:S(2)}, u32[]{:S(2)}) %collective-permute-start.1) | collective-permute-done | bytes 524320 | tf_op jit(solution)/shard_map/ppermute | solution.py:36
  35.8 2.1 %constant_dynamic-update-slice_fusion.13 = bf16[512,4096]{1,0:T(8,128)(2,1)} fusion(bf16[512,4096]{1,0:T(8,128)(2,1)} %constant_dynamic-update-slice_fusion.14, bf16[64,4096]{1,0:T(8,128)(2,1)} %copy-done.17), kind=kLoop, calls=%fused_computation.13 | loop fusion | bytes 1048576
  40.9 2.6 %collective-permute-done.13.refs_22_.refs_6_ = bf16[64,4096]{1,0:T(8,128)(2,1)S(1)} collective-permute-done((bf16[64,4096]{1,0:T(8,128)(2,1)S(1)}, bf16[64,4096]{1,0:T(8,128)(2,1)S(1)}, u32[]{:S(2)}, u32[]{:S(2)}) %collective-permute-start.13) | collective-permute-done | bytes 524320 | tf_op jit(solution)/shard_map/ppermute | solution.py:36
  43.5 3.1 %collective-permute-start.15 = (bf16[64,4096]{1,0:T(8,128)(2,1)S(1)}, bf16[64,4096]{1,0:T(8,128)(2,1)S(1)}, u32[]{:S(2)}, u32[]{:S(2)}) collective-permute-start(bf16[64,4096]{1,0:T(8,128)(2,1)S(1)} %collective-permute-done.13.refs_22_.refs_6_), channel_id=1, source_target_pairs={{0,16},{16,32},{32,48},{48,0},{64,80},{80,96},{96,112},{112,64},{1... | collective-permute-start | bytes 1572872 | tf_op jit(solution)/shard_map/ppermute | solution.py:36
  46.7 2.2 %collective-permute-done.8.refs_10_ = bf16[64,4096]{1,0:T(8,128)(2,1)S(1)} collective-permute-done((bf16[64,4096]{1,0:T(8,128)(2,1)S(1)}, bf16[64,4096]{1,0:T(8,128)(2,1)S(1)}, u32[]{:S(2)}, u32[]{:S(2)}) %collective-permute-start.8) | collective-permute-done | bytes 524320 | tf_op jit(solution)/shard_map/ppermute | solution.py:36
  48.9 3.8 %collective-permute-start.7 = (bf16[64,4096]{1,0:T(8,128)(2,1)S(1)}, bf16[64,4096]{1,0:T(8,128)(2,1)S(1)}, u32[]{:S(2)}, u32[]{:S(2)}) collective-permute-start(bf16[64,4096]{1,0:T(8,128)(2,1)S(1)} %collective-permute-done.5.refs_21_.refs_5_), channel_id=1, source_target_pairs={{0,16},{16,32},{32,48},{48,0},{64,80},{80,96},{96,112},{112,64},{1... | collective-permute-start | bytes 1572872 | tf_op jit(solution)/shard_map/ppermute | solution.py:36
  54.3 5.7 %collective-permute-done.9.refs_26_.refs_10_ = bf16[64,4096]{1,0:T(8,128)(2,1)S(1)} collective-permute-done((bf16[64,4096]{1,0:T(8,128)(2,1)S(1)}, bf16[64,4096]{1,0:T(8,128)(2,1)S(1)}, u32[]{:S(2)}, u32[]{:S(2)}) %collective-permute-start.9) | collective-permute-done | bytes 524320 | tf_op jit(solution)/shard_map/ppermute | solution.py:36
  60.1 3.8 %collective-permute-start.20 = (bf16[64,4096]{1,0:T(8,128)(2,1)S(1)}, bf16[64,4096]{1,0:T(8,128)(2,1)S(1)}, u32[]{:S(2)}, u32[]{:S(2)}) collective-permute-start(bf16[64,4096]{1,0:T(8,128)(2,1)S(1)} %collective-permute-done.9.refs_26_.refs_10_), channel_id=1, source_target_pairs={{0,16},{16,32},{32,48},{48,0},{64,80},{80,96},{96,112},{112,64},{1... | collective-permute-start | bytes 1572872 | tf_op jit(solution)/shard_map/ppermute | solution.py:36
  64.0 2.2 %constant_dynamic-update-slice_fusion.7 = bf16[512,4096]{1,0:T(8,128)(2,1)} fusion(bf16[64,4096]{1,0:T(8,128)(2,1)} %collective-permute-done.refs_9_), kind=kLoop, calls=%fused_computation.7 | loop fusion | bytes 1048576
  70.1 3.0 %collective-permute-start.21 = (bf16[64,4096]{1,0:T(8,128)(2,1)S(1)}, bf16[64,4096]{1,0:T(8,128)(2,1)S(1)}, u32[]{:S(2)}, u32[]{:S(2)}) collective-permute-start(bf16[64,4096]{1,0:T(8,128)(2,1)S(1)} %collective-permute-done.17.refs_12_), channel_id=1, source_target_pairs={{0,2},{1,7},{2,4},{3,1},{4,6},{5,3},{6,0},{7,5},{8,10},{9,15},{10,... | collective-permute-start | bytes 1572872 | tf_op jit(solution)/shard_map/ppermute | solution.py:36
  76.0 3.1 %collective-permute-start.22 = (bf16[64,4096]{1,0:T(8,128)(2,1)S(1)}, bf16[64,4096]{1,0:T(8,128)(2,1)S(1)}, u32[]{:S(2)}, u32[]{:S(2)}) collective-permute-start(bf16[64,4096]{1,0:T(8,128)(2,1)S(1)} %collective-permute-done.18.refs_27_.refs_11_), channel_id=1, source_target_pairs={{0,16},{16,32},{32,48},{48,0},{64,80},{80,96},{96,112},{112,64},{1... | collective-permute-start | bytes 1572872 | tf_op jit(solution)/shard_map/ppermute | solution.py:36
  83.1 2.0 %collective-permute-start.27 = (bf16[64,4096]{1,0:T(8,128)(2,1)S(1)}, bf16[64,4096]{1,0:T(8,128)(2,1)S(1)}, u32[]{:S(2)}, u32[]{:S(2)}) collective-permute-start(bf16[64,4096]{1,0:T(8,128)(2,1)S(1)} %collective-permute-done.24.refs_30_.refs_14_), channel_id=1, source_target_pairs={{0,16},{16,32},{32,48},{48,0},{64,80},{80,96},{96,112},{112,64},{1... | collective-permute-start | bytes 1572872 | tf_op jit(solution)/shard_map/ppermute | solution.py:36
  88.7 2.0 %collective-permute-start.26 = (bf16[64,4096]{1,0:T(8,128)(2,1)S(1)}, bf16[64,4096]{1,0:T(8,128)(2,1)S(1)}, u32[]{:S(2)}, u32[]{:S(2)}) collective-permute-start(bf16[64,4096]{1,0:T(8,128)(2,1)S(1)} %collective-permute-done.22.refs_29_.refs_13_), channel_id=1, source_target_pairs={{0,16},{16,32},{32,48},{48,0},{64,80},{80,96},{96,112},{112,64},{1... | collective-permute-start | bytes 1572872 | tf_op jit(solution)/shard_map/ppermute | solution.py:36
  92.3 4.9 %collective-permute-done.23.refs_15_ = bf16[64,4096]{1,0:T(8,128)(2,1)S(1)} collective-permute-done((bf16[64,4096]{1,0:T(8,128)(2,1)S(1)}, bf16[64,4096]{1,0:T(8,128)(2,1)S(1)}, u32[]{:S(2)}, u32[]{:S(2)}) %collective-permute-start.23) | collective-permute-done | bytes 524320 | tf_op jit(solution)/shard_map/ppermute | solution.py:36
  99.2 2.9 %collective-permute-start.28 = (bf16[512,4096]{1,0:T(8,128)(2,1)}, bf16[512,4096]{1,0:T(8,128)(2,1)}, u32[]{:S(2)}, u32[]{:S(2)}) collective-permute-start(bf16[512,4096]{1,0:T(8,128)(2,1)} %constant_dynamic-update-slice_fusion), channel_id=1, source_target_pairs={{0,1},{1,0},{2,3},{3,2},{4,5},{5,4},{6,7},{7,6},{8,9},{9,8},{10,11... | collective-permute-start | bytes 12582920 | tf_op jit(solution)/shard_map/ppermute | solution.py:36
  102.1 19.9 %shard_map.65.refs_17_ = f32[2048,2,4,128]{3,2,1,0:T(4,128)} custom-call(s32[42]{0:T(128)} %stack.171.number, bf16[64,4096]{1,0:T(8,128)(2,1)} %get-tuple-element.35.refs_0_, bf16[64,4096]{1,0:T(8,128)(2,1)} %get-tuple-element.42.refs_1_, bf16[64,4096]{1,0:T(8,128)(2,1)} %copy-done.17, bf16[64,4096]{1,0:T(8,128)(2,1)} %collective-permute-done.10.refs_3_, ...), custom_call_target="tpu_custom_call" | custom-call | flops 12884901888 | bytes 16777216 | tf_op jit(solution)/shard_map/pallas_call | solution.py:172
  122.0 10.4 %shard_map.66 = f32[2048,2,4,128]{3,2,1,0:T(4,128)} custom-call(s32[42]{0:T(128)} %stack.171.number, bf16[512,4096]{1,0:T(8,128)(2,1)} %collective-permute-done.28.refs_0_, bf16[64,4096]{1,0:T(8,128)(2,1)} %copy-done.1, bf16[64,4096]{1,0:T(8,128)(2,1)} %copy-done, bf16[64,4096]{1,0:T(8,128)(2,1)} %copy-done.2, ...), custom_call_target="tpu_custom_call", output_to_operand_aliasing={{}: (18, {})} | custom-call | flops 4294967296 | bytes 16777216 | tf_op jit(solution)/shard_map/pallas_call | solution.py:172
  (116 shorter events, 33.2 us)
Async XLA Ops:
  4.6 12.9 %collective-permute-start.2 = (bf16[64,4096]{1,0:T(8,128)(2,1)}, bf16[64,4096]{1,0:T(8,128)(2,1)S(1)}, u32[]{:S(2)}, u32[]{:S(2)}) collective-permute-start(bf16[64,4096]{1,0:T(8,128)(2,1)} %get-tuple-element.35.refs_0_), channel_id=1, source_target_pairs={{0,2},{1,7},{2,4},{3,1},{4,6},{5,3},{6,0},{7,5},{8,10},{9,15},{10,... | collective-permute-start | bytes 1572872 | tf_op jit(solution)/shard_map/ppermute | solution.py:36
  8.2 23.6 %collective-permute-start = (bf16[64,4096]{1,0:T(8,128)(2,1)}, bf16[64,4096]{1,0:T(8,128)(2,1)}, u32[]{:S(2)}, u32[]{:S(2)}) collective-permute-start(bf16[64,4096]{1,0:T(8,128)(2,1)} %get-tuple-element.35.refs_0_), channel_id=1, source_target_pairs={{0,8},{1,9},{2,10},{3,11},{4,12},{5,13},{6,14},{7,15},{8,0},{9,1},... | collective-permute-start | bytes 1572872 | tf_op jit(solution)/shard_map/ppermute | solution.py:36
  10.7 12.9 %collective-permute-start.3 = (bf16[64,4096]{1,0:T(8,128)(2,1)S(1)}, bf16[64,4096]{1,0:T(8,128)(2,1)S(1)}, u32[]{:S(2)}, u32[]{:S(2)}) collective-permute-start(bf16[64,4096]{1,0:T(8,128)(2,1)S(1)} %get-tuple-element.66.refs_17_.refs_1_), channel_id=1, source_target_pairs={{0,16},{16,32},{32,48},{48,0},{64,80},{80,96},{96,112},{112,64},{1... | collective-permute-start | bytes 1572872 | tf_op jit(solution)/shard_map/ppermute | solution.py:36
  14.6 21.2 %collective-permute-start.1 = (bf16[64,4096]{1,0:T(8,128)(2,1)S(1)}, bf16[64,4096]{1,0:T(8,128)(2,1)S(1)}, u32[]{:S(2)}, u32[]{:S(2)}) collective-permute-start(bf16[64,4096]{1,0:T(8,128)(2,1)S(1)} %get-tuple-element.66.refs_17_.refs_1_), channel_id=1, source_target_pairs={{0,64},{16,80},{32,96},{48,112},{64,0},{80,16},{96,32},{112,48},{1... | collective-permute-start | bytes 1572872 | tf_op jit(solution)/shard_map/ppermute | solution.py:36
  23.6 16.1 %collective-permute-start.4 = (bf16[64,4096]{1,0:T(8,128)(2,1)}, bf16[64,4096]{1,0:T(8,128)(2,1)S(1)}, u32[]{:S(2)}, u32[]{:S(2)}) collective-permute-start(bf16[64,4096]{1,0:T(8,128)(2,1)} %copy-done.17), channel_id=1, source_target_pairs={{0,2},{1,7},{2,4},{3,1},{4,6},{5,3},{6,0},{7,5},{8,10},{9,15},{10,... | collective-permute-start | bytes 1572872 | tf_op jit(solution)/shard_map/ppermute | solution.py:36
  26.7 14.2 %collective-permute-start.12 = (bf16[64,4096]{1,0:T(8,128)(2,1)}, bf16[64,4096]{1,0:T(8,128)(2,1)S(1)}, u32[]{:S(2)}, u32[]{:S(2)}) collective-permute-start(bf16[64,4096]{1,0:T(8,128)(2,1)} %collective-permute-done.10.refs_3_), channel_id=1, source_target_pairs={{0,2},{1,7},{2,4},{3,1},{4,6},{5,3},{6,0},{7,5},{8,10},{9,15},{10,... | collective-permute-start | bytes 1572872 | tf_op jit(solution)/shard_map/ppermute | solution.py:36
  28.4 12.5 %collective-permute-start.5 = (bf16[64,4096]{1,0:T(8,128)(2,1)S(1)}, bf16[64,4096]{1,0:T(8,128)(2,1)S(1)}, u32[]{:S(2)}, u32[]{:S(2)}) collective-permute-start(bf16[64,4096]{1,0:T(8,128)(2,1)S(1)} %collective-permute-done.3.refs_19_.refs_3_), channel_id=1, source_target_pairs={{0,16},{16,32},{32,48},{48,0},{64,80},{80,96},{96,112},{112,64},{1... | collective-permute-start | bytes 1572872 | tf_op jit(solution)/shard_map/ppermute | solution.py:36
  31.8 11.7 %collective-permute-start.13 = (bf16[64,4096]{1,0:T(8,128)(2,1)S(1)}, bf16[64,4096]{1,0:T(8,128)(2,1)S(1)}, u32[]{:S(2)}, u32[]{:S(2)}) collective-permute-start(bf16[64,4096]{1,0:T(8,128)(2,1)S(1)} %collective-permute-done.11.refs_20_.refs_4_), channel_id=1, source_target_pairs={{0,16},{16,32},{32,48},{48,0},{64,80},{80,96},{96,112},{112,64},{1... | collective-permute-start | bytes 1572872 | tf_op jit(solution)/shard_map/ppermute | solution.py:36
  35.8 13.1 %collective-permute-start.8 = (bf16[64,4096]{1,0:T(8,128)(2,1)S(1)}, bf16[64,4096]{1,0:T(8,128)(2,1)S(1)}, u32[]{:S(2)}, u32[]{:S(2)}) collective-permute-start(bf16[64,4096]{1,0:T(8,128)(2,1)S(1)} %copy-done.16), channel_id=1, source_target_pairs={{0,8},{1,9},{2,10},{3,11},{4,12},{5,13},{6,14},{7,15},{8,0},{9,1},... | collective-permute-start | bytes 1572872 | tf_op jit(solution)/shard_map/ppermute | solution.py:36
  39.7 20.3 %collective-permute-start.9 = (bf16[64,4096]{1,0:T(8,128)(2,1)S(1)}, bf16[64,4096]{1,0:T(8,128)(2,1)S(1)}, u32[]{:S(2)}, u32[]{:S(2)}) collective-permute-start(bf16[64,4096]{1,0:T(8,128)(2,1)S(1)} %get-tuple-element.43.refs_18_.refs_2_), channel_id=1, source_target_pairs={{0,64},{16,80},{32,96},{48,112},{64,0},{80,16},{96,32},{112,48},{1... | collective-permute-start | bytes 1572872 | tf_op jit(solution)/shard_map/ppermute | solution.py:36
  40.9 23.1 %collective-permute-start.6 = (bf16[64,4096]{1,0:T(8,128)(2,1)S(1)}, bf16[64,4096]{1,0:T(8,128)(2,1)S(1)}, u32[]{:S(2)}, u32[]{:S(2)}) collective-permute-start(bf16[64,4096]{1,0:T(8,128)(2,1)S(1)} %collective-permute-done.4.refs_4_), channel_id=1, source_target_pairs={{0,2},{1,7},{2,4},{3,1},{4,6},{5,3},{6,0},{7,5},{8,10},{9,15},{10,... | collective-permute-start | bytes 1572872 | tf_op jit(solution)/shard_map/ppermute | solution.py:36
  43.5 16.5 %collective-permute-start.14 = (bf16[64,4096]{1,0:T(8,128)(2,1)S(1)}, bf16[64,4096]{1,0:T(8,128)(2,1)S(1)}, u32[]{:S(2)}, u32[]{:S(2)}) collective-permute-start(bf16[64,4096]{1,0:T(8,128)(2,1)S(1)} %collective-permute-done.12.refs_5_), channel_id=1, source_target_pairs={{0,2},{1,7},{2,4},{3,1},{4,6},{5,3},{6,0},{7,5},{8,10},{9,15},{10,... | collective-permute-start | bytes 1572872 | tf_op jit(solution)/shard_map/ppermute | solution.py:36
  43.5 16.5 %collective-permute-start.15 = (bf16[64,4096]{1,0:T(8,128)(2,1)S(1)}, bf16[64,4096]{1,0:T(8,128)(2,1)S(1)}, u32[]{:S(2)}, u32[]{:S(2)}) collective-permute-start(bf16[64,4096]{1,0:T(8,128)(2,1)S(1)} %collective-permute-done.13.refs_22_.refs_6_), channel_id=1, source_target_pairs={{0,16},{16,32},{32,48},{48,0},{64,80},{80,96},{96,112},{112,64},{1... | collective-permute-start | bytes 1572872 | tf_op jit(solution)/shard_map/ppermute | solution.py:36
  48.9 15.1 %collective-permute-start.7 = (bf16[64,4096]{1,0:T(8,128)(2,1)S(1)}, bf16[64,4096]{1,0:T(8,128)(2,1)S(1)}, u32[]{:S(2)}, u32[]{:S(2)}) collective-permute-start(bf16[64,4096]{1,0:T(8,128)(2,1)S(1)} %collective-permute-done.5.refs_21_.refs_5_), channel_id=1, source_target_pairs={{0,16},{16,32},{32,48},{48,0},{64,80},{80,96},{96,112},{112,64},{1... | collective-permute-start | bytes 1572872 | tf_op jit(solution)/shard_map/ppermute | solution.py:36
  60.0 10.0 %collective-permute-start.17 = (bf16[64,4096]{1,0:T(8,128)(2,1)S(1)}, bf16[64,4096]{1,0:T(8,128)(2,1)S(1)}, u32[]{:S(2)}, u32[]{:S(2)}) collective-permute-start(bf16[64,4096]{1,0:T(8,128)(2,1)S(1)} %collective-permute-done.8.refs_10_), channel_id=1, source_target_pairs={{0,2},{1,7},{2,4},{3,1},{4,6},{5,3},{6,0},{7,5},{8,10},{9,15},{10,... | collective-permute-start | bytes 1572872 | tf_op jit(solution)/shard_map/ppermute | solution.py:36
  68.0 34.0 %collective-permute-start.29 = (bf16[512,4096]{1,0:T(8,128)(2,1)}, bf16[512,4096]{1,0:T(8,128)(2,1)}, u32[]{:S(2)}, u32[]{:S(2)}) collective-permute-start(bf16[512,4096]{1,0:T(8,128)(2,1)} %constant_dynamic-update-slice_fusion.8), channel_id=1, source_target_pairs={{0,1},{1,0},{2,3},{3,2},{4,5},{5,4},{6,7},{7,6},{8,9},{9,8},{10,11... | collective-permute-start | bytes 12582920 | tf_op jit(solution)/shard_map/ppermute | solution.py:36
  70.1 10.7 %collective-permute-start.21 = (bf16[64,4096]{1,0:T(8,128)(2,1)S(1)}, bf16[64,4096]{1,0:T(8,128)(2,1)S(1)}, u32[]{:S(2)}, u32[]{:S(2)}) collective-permute-start(bf16[64,4096]{1,0:T(8,128)(2,1)S(1)} %collective-permute-done.17.refs_12_), channel_id=1, source_target_pairs={{0,2},{1,7},{2,4},{3,1},{4,6},{5,3},{6,0},{7,5},{8,10},{9,15},{10,... | collective-permute-start | bytes 1572872 | tf_op jit(solution)/shard_map/ppermute | solution.py:36
  75.7 10.3 %collective-permute-start.19 = (bf16[64,4096]{1,0:T(8,128)(2,1)S(1)}, bf16[64,4096]{1,0:T(8,128)(2,1)S(1)}, u32[]{:S(2)}, u32[]{:S(2)}) collective-permute-start(bf16[64,4096]{1,0:T(8,128)(2,1)S(1)} %collective-permute-done.16.refs_11_), channel_id=1, source_target_pairs={{0,2},{1,7},{2,4},{3,1},{4,6},{5,3},{6,0},{7,5},{8,10},{9,15},{10,... | collective-permute-start | bytes 1572872 | tf_op jit(solution)/shard_map/ppermute | solution.py:36
  76.0 11.0 %collective-permute-start.22 = (bf16[64,4096]{1,0:T(8,128)(2,1)S(1)}, bf16[64,4096]{1,0:T(8,128)(2,1)S(1)}, u32[]{:S(2)}, u32[]{:S(2)}) collective-permute-start(bf16[64,4096]{1,0:T(8,128)(2,1)S(1)} %collective-permute-done.18.refs_27_.refs_11_), channel_id=1, source_target_pairs={{0,16},{16,32},{32,48},{48,0},{64,80},{80,96},{96,112},{112,64},{1... | collective-permute-start | bytes 1572872 | tf_op jit(solution)/shard_map/ppermute | solution.py:36
  81.4 16.7 %collective-permute-start.25 = (bf16[64,4096]{1,0:T(8,128)(2,1)S(1)}, bf16[64,4096]{1,0:T(8,128)(2,1)S(1)}, u32[]{:S(2)}, u32[]{:S(2)}) collective-permute-start(bf16[64,4096]{1,0:T(8,128)(2,1)S(1)} %collective-permute-done.21.refs_14_), channel_id=1, source_target_pairs={{0,2},{1,7},{2,4},{3,1},{4,6},{5,3},{6,0},{7,5},{8,10},{9,15},{10,... | collective-permute-start | bytes 1572872 | tf_op jit(solution)/shard_map/ppermute | solution.py:36
  83.1 16.0 %collective-permute-start.27 = (bf16[64,4096]{1,0:T(8,128)(2,1)S(1)}, bf16[64,4096]{1,0:T(8,128)(2,1)S(1)}, u32[]{:S(2)}, u32[]{:S(2)}) collective-permute-start(bf16[64,4096]{1,0:T(8,128)(2,1)S(1)} %collective-permute-done.24.refs_30_.refs_14_), channel_id=1, source_target_pairs={{0,16},{16,32},{32,48},{48,0},{64,80},{80,96},{96,112},{112,64},{1... | collective-permute-start | bytes 1572872 | tf_op jit(solution)/shard_map/ppermute | solution.py:36
  87.1 10.2 %collective-permute-start.23 = (bf16[64,4096]{1,0:T(8,128)(2,1)S(1)}, bf16[64,4096]{1,0:T(8,128)(2,1)S(1)}, u32[]{:S(2)}, u32[]{:S(2)}) collective-permute-start(bf16[64,4096]{1,0:T(8,128)(2,1)S(1)} %collective-permute-done.19.refs_13_), channel_id=1, source_target_pairs={{0,2},{1,7},{2,4},{3,1},{4,6},{5,3},{6,0},{7,5},{8,10},{9,15},{10,... | collective-permute-start | bytes 1572872 | tf_op jit(solution)/shard_map/ppermute | solution.py:36
  88.7 10.4 %collective-permute-start.26 = (bf16[64,4096]{1,0:T(8,128)(2,1)S(1)}, bf16[64,4096]{1,0:T(8,128)(2,1)S(1)}, u32[]{:S(2)}, u32[]{:S(2)}) collective-permute-start(bf16[64,4096]{1,0:T(8,128)(2,1)S(1)} %collective-permute-done.22.refs_29_.refs_13_), channel_id=1, source_target_pairs={{0,16},{16,32},{32,48},{48,0},{64,80},{80,96},{96,112},{112,64},{1... | collective-permute-start | bytes 1572872 | tf_op jit(solution)/shard_map/ppermute | solution.py:36
  99.2 22.9 %collective-permute-start.28 = (bf16[512,4096]{1,0:T(8,128)(2,1)}, bf16[512,4096]{1,0:T(8,128)(2,1)}, u32[]{:S(2)}, u32[]{:S(2)}) collective-permute-start(bf16[512,4096]{1,0:T(8,128)(2,1)} %constant_dynamic-update-slice_fusion), channel_id=1, source_target_pairs={{0,1},{1,0},{2,3},{3,2},{4,5},{5,4},{6,7},{7,6},{8,9},{9,8},{10,11... | collective-permute-start | bytes 12582920 | tf_op jit(solution)/shard_map/ppermute | solution.py:36
  (35 other events, 840.2 us)
